TPU v7x, 32 devices: a whole 2x2x4 slice. The times are simulated.
32 devices in a mesh: dp: 4 (over x, core), seq: 8 (over z, y).
Axes of the slice: x: 2, y: 2, z: 4, core: 2. Of those that a mesh axis runs over, the one named last changes fastest.
Arguments:
- tokens: bfloat16 [4, 2048, 1536], P('dp', 'seq'), may hold values from -6 to 6
- segment_ids: int32 [4, 2048], P('dp', 'seq'), may hold values from 0 to 4, as said below
- pre_gain: bfloat16 [1536], P(('dp', 'seq')), may hold values from 0.5 to 1.5
- in_weight: bfloat16 [1536, 6448], P(('dp', 'seq')), may hold values from -0.15625 to 0.15625
- conv_weight: bfloat16 [3328, 4], P(('dp', 'seq')), may hold values from -3 to 3
- conv_bias: bfloat16 [3328], P(('dp', 'seq')), may hold values from -3 to 3
- dt_bias: float32 [48], replicated, may hold values from -5 to -1
- a_log: float32 [48], replicated, may hold values from -10 to 0
- skip_gain: float32 [48], replicated, may hold values from 0.5 to 1.5
- norm_gain: bfloat16 [3072], P(('dp', 'seq')), may hold values from 0.5 to 1.5
- out_weight: bfloat16 [3072, 1536], P(('dp', 'seq')), may hold values from -0.109375 to 0.109375
- cotangent: bfloat16 [4, 2048, 1536], P('dp', 'seq'), may hold values from -6 to 6
Outputs:
- mixed: bfloat16 [4, 2048, 1536], P('dp', 'seq')
- tokens_grad: float32 [4, 2048, 1536], P('dp', 'seq')
- pre_gain_grad: float32 [1536], P(('dp', 'seq'))
- in_weight_grad: float32 [1536, 6448], P(('dp', 'seq'))
- conv_weight_grad: float32 [3328, 4], P(('dp', 'seq'))
- conv_bias_grad: float32 [3328], P(('dp', 'seq'))
- dt_bias_grad: float32 [48], replicated
- a_log_grad: float32 [48], replicated
- skip_grad: float32 [48], replicated
- norm_gain_grad: float32 [3072], P(('dp', 'seq'))
- out_weight_grad: float32 [3072, 1536], P(('dp', 'seq'))
Inputs may be any that keep to these rules, and one draw needn't show every extreme that they name: `segment_ids`: along each sequence the ids never fall, start at 0 and rise by one at each document start.
All inputs are finite; a program needn't handle non-finite values.
Results may differ from a plain program's by a relative error of at most 0.0069.
Values may be sent and summed in bfloat16 or wider, within the bound.
A program may use at most 256 MiB of HBM per device.

v0:
```python
import jax
import jax.numpy as jnp
from jax import lax
from jax.sharding import PartitionSpec as P

HEADS = 48
HEADDIM = 64
STATE = 128
CONVW = 4
GROUP = 256
INNER = 3072
XBC = 3328


HIGHEST = lax.Precision.HIGHEST
EPSILON = 1e-05


def passed_along(block, axis, distance):
    devices = range(lax.axis_size(axis))
    route = [(i - distance, i) for i in devices if i - distance in devices]
    return lax.ppermute(block, axis, route)


def shortened(shard):
    return jax.tree.map(lambda a: a.astype(jnp.bfloat16) if a.dtype == jnp.float32 else a, shard)


def rms_scale(values, gain):
    return values * lax.rsqrt(jnp.mean(values * values, axis=-1, keepdims=True) + EPSILON) * gain


def gating(values, gates, gain):
    return rms_scale(values * jax.nn.silu(gates), gain)


def group_math(state, before, heads_x, b_rows, c_rows, steps_dt, log_decay, doc_ids):
    length = doc_ids.shape[0]
    running = jnp.cumsum(log_decay, axis=0)
    causal = jnp.arange(length)[:, None] >= jnp.arange(length)[None, :]
    linked = ((doc_ids[:, None] == doc_ids[None, :]) & causal)[:, :, None]
    gaps = running[:, None, :] - running[None, :, :]
    decays = jnp.exp(jnp.where(linked, gaps, 0.0)) * linked
    scores = jnp.dot(c_rows, b_rows.T, precision=HIGHEST)
    mixing = decays * scores[:, :, None] * steps_dt[None, :, :]
    inside = jnp.einsum("tsh,shp->thp", mixing, heads_x, precision=HIGHEST)
    alive = (doc_ids == before)[:, None]
    enter = jnp.exp(running) * alive
    carried = jnp.einsum("tn,hpn->thp", c_rows, state, precision=HIGHEST) * enter[:, :, None]
    last_id = doc_ids[length - 1]
    kept = (doc_ids == last_id)[:, None]
    weights_end = jnp.exp(running[length - 1][None, :] - running) * kept * steps_dt
    fresh = jnp.einsum("sh,shp,sn->hpn", weights_end, heads_x, b_rows, precision=HIGHEST)
    passed = jnp.exp(running[length - 1]) * (last_id == before)
    return (inside + carried, fresh + passed[:, None, None] * state)


def contract_rows(left, right):
    return lax.dot_general(
        left, right, (((0,), (0,)), ((), ())), preferred_element_type=jnp.float32
    )


def contract_cols(left, right):
    return lax.dot_general(
        left, right, (((1,), (1,)), ((), ())), preferred_element_type=jnp.float32
    )


def body(
    tokens,
    segment_ids,
    pre_gain,
    in_weight,
    conv_weight,
    conv_bias,
    dt_bias,
    a_log,
    skip_gain,
    norm_gain,
    out_weight,
    cotangent,
):
    tok_rows = tokens[0].astype(jnp.float32)
    doc_ids = segment_ids[0]
    length = doc_ids.shape[0]
    margin = CONVW - 1
    count = length // GROUP
    shards = (pre_gain, in_weight, conv_weight, conv_bias, norm_gain, out_weight)
    gathered = (
        lax.all_gather(shards[0], ("dp", "seq"), axis=0, tiled=True),
        lax.all_gather(shards[1], ("dp", "seq"), axis=0, tiled=True),
        lax.all_gather(shards[2], ("dp", "seq"), axis=0, tiled=True),
        lax.all_gather(shards[3], ("dp", "seq"), axis=0, tiled=True),
        lax.all_gather(shards[4], ("dp", "seq"), axis=0, tiled=True),
        lax.all_gather(shards[5], ("dp", "seq"), axis=0, tiled=True),
    )
    normed, pre_back = jax.vjp(rms_scale, tok_rows, gathered[0].astype(jnp.float32))
    normed_low = normed.astype(jnp.bfloat16)
    projected = jnp.dot(normed_low, gathered[1], preferred_element_type=jnp.float32)
    gate_z = projected[:, :INNER]
    conv_in = projected[:, INNER : INNER + XBC]
    dt_raw = projected[:, INNER + XBC :]
    halo_rows, halo_ids = (
        passed_along(conv_in[length - margin :].astype(jnp.bfloat16), "seq", 1).astype(jnp.float32),
        passed_along(
            doc_ids[length - margin :].astype(jnp.float32).astype(jnp.bfloat16), "seq", 1
        ).astype(jnp.float32),
    )
    ext_ids = jnp.concatenate([halo_ids.astype(jnp.int32), doc_ids])
    prior_id = ext_ids[margin - 1]

    def convolve(extended, kernel, offset_bias):
        total = offset_bias
        for offset in range(CONVW):
            taps = extended[offset : offset + length]
            linked = (ext_ids[offset : offset + length] == doc_ids)[:, None]
            total = total + jnp.where(linked, taps, 0.0) * kernel[:, offset]
        return jax.nn.silu(total)

    activated, conv_back = jax.vjp(
        convolve,
        jnp.concatenate([halo_rows, conv_in]),
        gathered[2].astype(jnp.float32),
        gathered[3].astype(jnp.float32),
    )

    def zero_state(acts_in, raw_in, shift_in, rate_in):
        heads_x = acts_in[:, :INNER].reshape(length, HEADS, HEADDIM)
        b_rows = acts_in[:, INNER : INNER + STATE]
        c_rows = acts_in[:, INNER + STATE :]
        steps_dt = jax.nn.softplus(raw_in + shift_in)
        log_decay = -jnp.exp(rate_in) * steps_dt
        befores = jnp.concatenate([prior_id[None], doc_ids.reshape(count, GROUP)[:-1, GROUP - 1]])

        def step(state, item):
            out, new_state = group_math(state, *item)
            return (new_state, out)

        items = (
            befores,
            heads_x.reshape(count, GROUP, HEADS, HEADDIM),
            b_rows.reshape(count, GROUP, STATE),
            c_rows.reshape(count, GROUP, STATE),
            steps_dt.reshape(count, GROUP, HEADS),
            log_decay.reshape(count, GROUP, HEADS),
            doc_ids.reshape(count, GROUP),
        )
        final, outs = lax.scan(step, jnp.zeros((HEADS, HEADDIM, STATE), jnp.float32), items)
        factor = jnp.exp(jnp.sum(log_decay, axis=0)) * (doc_ids[length - 1] == prior_id)
        return (outs.reshape(length, HEADS, HEADDIM), factor, final)

    def incoming(acts_in, raw_in, shift_in, rate_in, start_state):
        steps_dt = jax.nn.softplus(raw_in + shift_in)
        running = jnp.cumsum(-jnp.exp(rate_in) * steps_dt, axis=0)
        factor = jnp.exp(running) * (doc_ids == prior_id)[:, None]
        c_rows = acts_in[:, INNER + STATE :]
        return (
            jnp.einsum("tn,hpn->thp", c_rows, start_state, precision=HIGHEST) * factor[:, :, None]
        )

    (local_y, factor, local_state), zero_back = jax.vjp(
        zero_state, activated, dt_raw, dt_bias, a_log
    )
    identity = (jnp.ones((HEADS,), jnp.float32), jnp.zeros((HEADS, HEADDIM, STATE), jnp.float32))

    def forward_turn(index, carry_state):
        return passed_along(factor[:, None, None] * carry_state + local_state, "seq", 1)

    start_state = lax.fori_loop(0, lax.axis_size("seq") - 1, forward_turn, identity[1])
    carried_y, in_back = jax.vjp(incoming, activated, dt_raw, dt_bias, a_log, start_state)
    heads_x = activated[:, :INNER].reshape(length, HEADS, HEADDIM)
    mixer_out = (local_y + carried_y + skip_gain[:, None] * heads_x).reshape(length, INNER)
    gated, gate_back = jax.vjp(gating, mixer_out, gate_z, gathered[4].astype(jnp.float32))
    gated_low = gated.astype(jnp.bfloat16)
    branch = jnp.dot(gated_low, gathered[5], preferred_element_type=jnp.float32)
    mixed = (tok_rows + branch).astype(jnp.bfloat16)
    again = (
        lax.all_gather(shards[0], ("dp", "seq"), axis=0, tiled=True),
        lax.all_gather(shards[1], ("dp", "seq"), axis=0, tiled=True),
        lax.all_gather(shards[2], ("dp", "seq"), axis=0, tiled=True),
        lax.all_gather(shards[3], ("dp", "seq"), axis=0, tiled=True),
        lax.all_gather(shards[4], ("dp", "seq"), axis=0, tiled=True),
        lax.all_gather(shards[5], ("dp", "seq"), axis=0, tiled=True),
    )
    grad_out = cotangent[0]
    grad_gated = contract_cols(grad_out, again[5])
    out_weight_grad = contract_rows(gated_low, grad_out)
    grad_mixer, grad_gate_z, norm_gain_grad = gate_back(grad_gated)
    grad_heads = grad_mixer.reshape(length, HEADS, HEADDIM)
    skip_grad = jnp.sum(grad_heads * heads_x, axis=(0, 2))
    acts_one, raw_one, shift_one, rate_one, start_grad = in_back(grad_heads)

    def backward_turn(index, carry_grad):
        return passed_along(start_grad + factor[:, None, None] * carry_grad, "seq", -1)

    end_grad = lax.fori_loop(0, lax.axis_size("seq") - 1, backward_turn, identity[1])
    factor_grad = jnp.sum(end_grad * start_state, axis=(1, 2))
    acts_two, raw_two, shift_two, rate_two = zero_back((grad_heads, factor_grad, end_grad))
    skip_part = (grad_heads * skip_gain[:, None]).reshape(length, INNER)
    grad_acts = (
        acts_one
        + acts_two
        + jnp.concatenate([skip_part, jnp.zeros((length, 2 * STATE), jnp.float32)], axis=1)
    )
    grad_ext, conv_weight_grad, conv_bias_grad = conv_back(grad_acts)
    back_rows = passed_along(shortened(grad_ext[:margin]), "seq", -1)
    grad_conv_in = grad_ext[margin:] + jnp.concatenate(
        [jnp.zeros((length - margin, XBC), jnp.float32), back_rows]
    )
    grad_projected = jnp.concatenate([grad_gate_z, grad_conv_in, raw_one + raw_two], axis=1).astype(
        jnp.bfloat16
    )
    in_weight_grad = contract_rows(normed_low, grad_projected)
    grad_normed = contract_cols(grad_projected, again[1])
    grad_tokens_norm, pre_gain_grad = pre_back(grad_normed)
    tokens_grad = grad_out.astype(jnp.float32) + grad_tokens_norm
    grad_parts = (
        pre_gain_grad,
        in_weight_grad,
        conv_weight_grad,
        conv_bias_grad,
        norm_gain_grad,
        out_weight_grad,
    )
    row_sums = (
        lax.psum_scatter(grad_parts[0], "dp", scatter_dimension=0, tiled=True),
        lax.psum_scatter(grad_parts[1], "dp", scatter_dimension=0, tiled=True),
        lax.psum_scatter(grad_parts[2], "dp", scatter_dimension=0, tiled=True),
        lax.psum_scatter(grad_parts[3], "dp", scatter_dimension=0, tiled=True),
        lax.psum_scatter(grad_parts[4], "dp", scatter_dimension=0, tiled=True),
        lax.psum_scatter(grad_parts[5], "dp", scatter_dimension=0, tiled=True),
    )
    sums = (
        lax.psum_scatter(row_sums[0], "seq", scatter_dimension=0, tiled=True),
        lax.psum_scatter(row_sums[1], "seq", scatter_dimension=0, tiled=True),
        lax.psum_scatter(row_sums[2], "seq", scatter_dimension=0, tiled=True),
        lax.psum_scatter(row_sums[3], "seq", scatter_dimension=0, tiled=True),
        lax.psum_scatter(row_sums[4], "seq", scatter_dimension=0, tiled=True),
        lax.psum_scatter(row_sums[5], "seq", scatter_dimension=0, tiled=True),
    )
    head_sums = lax.psum((shift_one + shift_two, rate_one + rate_two, skip_grad), ("dp", "seq"))
    return (
        mixed[None],
        tokens_grad[None],
        sums[0],
        sums[1],
        sums[2],
        sums[3],
        head_sums[0],
        head_sums[1],
        head_sums[2],
        sums[4],
        sums[5],
    )


def solution(mesh):
    return jax.shard_map(
        body,
        mesh=mesh,
        in_specs=(
            P("dp", "seq", None),
            P("dp", "seq"),
            P(("dp", "seq")),
            P(("dp", "seq"), None),
            P(("dp", "seq"), None),
            P(("dp", "seq")),
            P(),
            P(),
            P(),
            P(("dp", "seq")),
            P(("dp", "seq"), None),
            P("dp", "seq", None),
        ),
        out_specs=(
            P("dp", "seq", None),
            P("dp", "seq", None),
            P(("dp", "seq")),
            P(("dp", "seq"), None),
            P(("dp", "seq"), None),
            P(("dp", "seq")),
            P(),
            P(),
            P(),
            P(("dp", "seq")),
            P(("dp", "seq"), None),
        ),
        check_vma=False,
    )
```

profile of v0, /device:TPU:1, one launch (start us, length us, event | category | flops | bytes accessed | tf_op | source)
XLA Modules:
  0.0 1506.5 jit_solution(7753642614696038516)
XLA Ops:
  17.2 42.2 %all-reduce.29 = (bf16[1536]{0:T(1024)(128)(2,1)S(1)}, bf16[3328]{0:T(1024)(128)(2,1)S(1)}, bf16[3072]{0:T(1024)(128)(2,1)S(1)}) all-reduce(bf16[1536]{0:T(1024)(128)(2,1)S(1)} %dynamic-update-slice.1, bf16[3328]{0:T(1024)(128)(2,1)S(1)} %dynamic-update-slice, ...), channel_id=1, replica_groups=mesh['dp'=4,'seq'=8] {'dp','seq'}, use_global_device_ids=true, to_apply=%add.17 | all-reduce | flops 7936 | bytes 31744
  59.4 61.7 %all-gather = bf16[32,104,4]{1,2,0:T(4,128)(2,1)S(1)} all-gather(bf16[1,104,4]{1,2,0:T(4,128)(2,1)} %bitcast.190), channel_id=1, replica_groups=mesh['dp'=4,'seq'=8] {'dp','seq'}, dimensions={0}, use_global_device_ids=true | all-gather | bytes 27456 | tf_op jit(solution)/shard_map/all_gather | solution.py:93
  131.4 13.7 all-gather.4.cloned.1.call-done
  145.1 13.0 fusion.92
  181.5 10.2 fusion.32
  193.6 4.3 fusion.88
  200.7 275.4 %while.4 = (s32[]{:T(128)}, f32[48,64,128]{2,1,0:T(8,128)S(1)}, f32[48]{0:T(128)S(1)}, f32[48,64,128]{2,1,0:T(8,128)S(1)}, s32[]{:T(128)}) while((s32[]{:T(128)}, f32[48,64,128]{2,1,0:T(8,128)S(1)}, f32[48]{0:T(128)S(1)}, f32[48,64,128]{2,1,0:T(8,128)S(1)}, s32[]{:T(128)}) %tuple.101), condition=%wide.region_5.7_spmd, body=%wide.region_4.6_spmd.sunk | while | flops 786434 | bytes 11010341 | solution.py:170
  203.5 42.3 %collective-permute-done = f32[48,64,128]{2,1,0:T(8,128)S(1)} collective-permute-done((f32[48,64,128]{2,1,0:T(8,128)}, f32[48,64,128]{2,1,0:T(8,128)S(1)}, u32[]{:S(2)}, u32[]{:S(2)}) %collective-permute-start) | collective-permute-done | bytes 1572896 | tf_op jit(solution)/shard_map/while/body/eval_jaxpr/ppermute | solution.py:22
  247.2 11.7 collective-permute-start
  258.9 33.2 %collective-permute-done = f32[48,64,128]{2,1,0:T(8,128)S(1)} collective-permute-done((f32[48,64,128]{2,1,0:T(8,128)}, f32[48,64,128]{2,1,0:T(8,128)S(1)}, u32[]{:S(2)}, u32[]{:S(2)}) %collective-permute-start) | collective-permute-done | bytes 1572896 | tf_op jit(solution)/shard_map/while/body/eval_jaxpr/ppermute | solution.py:22
  293.5 5.0 collective-permute-start
  298.5 32.3 %collective-permute-done = f32[48,64,128]{2,1,0:T(8,128)S(1)} collective-permute-done((f32[48,64,128]{2,1,0:T(8,128)}, f32[48,64,128]{2,1,0:T(8,128)S(1)}, u32[]{:S(2)}, u32[]{:S(2)}) %collective-permute-start) | collective-permute-done | bytes 1572896 | tf_op jit(solution)/shard_map/while/body/eval_jaxpr/ppermute | solution.py:22
  332.1 5.0 collective-permute-start
  337.1 31.4 %collective-permute-done = f32[48,64,128]{2,1,0:T(8,128)S(1)} collective-permute-done((f32[48,64,128]{2,1,0:T(8,128)}, f32[48,64,128]{2,1,0:T(8,128)S(1)}, u32[]{:S(2)}, u32[]{:S(2)}) %collective-permute-start) | collective-permute-done | bytes 1572896 | tf_op jit(solution)/shard_map/while/body/eval_jaxpr/ppermute | solution.py:22
  369.8 5.0 collective-permute-start
  374.8 30.4 %collective-permute-done = f32[48,64,128]{2,1,0:T(8,128)S(1)} collective-permute-done((f32[48,64,128]{2,1,0:T(8,128)}, f32[48,64,128]{2,1,0:T(8,128)S(1)}, u32[]{:S(2)}, u32[]{:S(2)}) %collective-permute-start) | collective-permute-done | bytes 1572896 | tf_op jit(solution)/shard_map/while/body/eval_jaxpr/ppermute | solution.py:22
  406.6 5.0 collective-permute-start
  411.6 29.5 %collective-permute-done = f32[48,64,128]{2,1,0:T(8,128)S(1)} collective-permute-done((f32[48,64,128]{2,1,0:T(8,128)}, f32[48,64,128]{2,1,0:T(8,128)S(1)}, u32[]{:S(2)}, u32[]{:S(2)}) %collective-permute-start) | collective-permute-done | bytes 1572896 | tf_op jit(solution)/shard_map/while/body/eval_jaxpr/ppermute | solution.py:22
  442.5 5.0 collective-permute-start
  447.5 28.6 %collective-permute-done = f32[48,64,128]{2,1,0:T(8,128)S(1)} collective-permute-done((f32[48,64,128]{2,1,0:T(8,128)}, f32[48,64,128]{2,1,0:T(8,128)S(1)}, u32[]{:S(2)}, u32[]{:S(2)}) %collective-permute-start) | collective-permute-done | bytes 1572896 | tf_op jit(solution)/shard_map/while/body/eval_jaxpr/ppermute | solution.py:22
  480.0 17.3 %fusion.37 = f32[256,48,64]{0,2,1:T(8,128)S(1)} fusion(f32[256,48,64]{0,2,1:T(8,128)S(1)} %bitcast.176, f32[256,48,64]{0,2,1:T(8,128)S(1)} %fusion.105, f32[256,48,64]{0,2,1:T(8,128)} %fusion.88, f32[256,48]{0,1:T(8,128)S(1)} %copy-done.60, f32[256,256]{1,0:T(8,128)S(1)} %copy-done.46, f32[256,256]{1,0:T(8,128)S(1)} %copy-done.44, ...), kind=kOutput, calls=%fused_computation.66 | convolution fusion | flops 2436366336 | bytes 13320384 | tf_op jit(solution)/shard_map/jvp()/while/body/eval_jaxpr/tsh,shp->thp/dot_general | solution.py:46
  503.1 8.1 fusion.83
  512.0 8.5 multiply_reduce_fusion.6
  520.6 6.3 multiply_reduce_fusion.7
  532.5 23.2 %fusion.9 = (f32[256,48]{0,1:T(8,128)S(1)}, f32[256,48]{0,1:T(8,128)S(1)}, f32[256,48]{0,1:T(8,128)}, f32[256,256]{1,0:T(8,128)}) fusion(f32[256,48]{0,1:T(8,128)S(1)} %copy-done.60, f32[256,256]{1,0:T(8,128)S(1)} %copy-done.46, f32[256,256]{1,0:T(8,128)S(1)} %copy-done.44, f32[256,48]{0,1:T(8,128)S(1)} %copy-done.58, pred[256,256]{1,0:T(8,128)(4,1)S(1)} %copy-done.50, ...), kind=kOutput, calls=%fused_computation.14 | convolution fusion | flops 2463002624 | bytes 7389184 | tf_op jit(solution)/shard_map/transpose(jvp())/while/body/eval_jaxpr/tsh,shp->thp/dot_general | solution.py:46
  557.9 5.8 fusion.43
  563.9 235.8 %while.5 = (s32[]{:T(128)}, f32[48,64,128]{2,1,0:T(8,128)S(1)}, f32[48]{0:T(128)S(1)}, f32[48,64,128]{2,1,0:T(8,128)}, s32[]{:T(128)}) while((s32[]{:T(128)}, f32[48,64,128]{2,1,0:T(8,128)S(1)}, f32[48]{0:T(128)S(1)}, f32[48,64,128]{2,1,0:T(8,128)}, s32[]{:T(128)}) %tuple.121), condition=%wide.region_10.12_spmd, body=%wide.region_9.11_spmd.sunk | while | flops 786434 | bytes 11010341 | solution.py:197
  568.0 32.0 %collective-permute-done.1 = f32[48,64,128]{2,1,0:T(8,128)S(1)} collective-permute-done((f32[48,64,128]{2,1,0:T(8,128)}, f32[48,64,128]{2,1,0:T(8,128)S(1)}, u32[]{:S(2)}, u32[]{:S(2)}) %collective-permute-start.1) | collective-permute-done | bytes 1572896 | tf_op jit(solution)/shard_map/while/body/eval_jaxpr/ppermute | solution.py:22
  604.0 30.8 %collective-permute-done.1 = f32[48,64,128]{2,1,0:T(8,128)S(1)} collective-permute-done((f32[48,64,128]{2,1,0:T(8,128)}, f32[48,64,128]{2,1,0:T(8,128)S(1)}, u32[]{:S(2)}, u32[]{:S(2)}) %collective-permute-start.1) | collective-permute-done | bytes 1572896 | tf_op jit(solution)/shard_map/while/body/eval_jaxpr/ppermute | solution.py:22
  638.9 29.3 %collective-permute-done.1 = f32[48,64,128]{2,1,0:T(8,128)S(1)} collective-permute-done((f32[48,64,128]{2,1,0:T(8,128)}, f32[48,64,128]{2,1,0:T(8,128)S(1)}, u32[]{:S(2)}, u32[]{:S(2)}) %collective-permute-start.1) | collective-permute-done | bytes 1572896 | tf_op jit(solution)/shard_map/while/body/eval_jaxpr/ppermute | solution.py:22
  672.3 28.8 %collective-permute-done.1 = f32[48,64,128]{2,1,0:T(8,128)S(1)} collective-permute-done((f32[48,64,128]{2,1,0:T(8,128)}, f32[48,64,128]{2,1,0:T(8,128)S(1)}, u32[]{:S(2)}, u32[]{:S(2)}) %collective-permute-start.1) | collective-permute-done | bytes 1572896 | tf_op jit(solution)/shard_map/while/body/eval_jaxpr/ppermute | solution.py:22
  705.2 28.8 %collective-permute-done.1 = f32[48,64,128]{2,1,0:T(8,128)S(1)} collective-permute-done((f32[48,64,128]{2,1,0:T(8,128)}, f32[48,64,128]{2,1,0:T(8,128)S(1)}, u32[]{:S(2)}, u32[]{:S(2)}) %collective-permute-start.1) | collective-permute-done | bytes 1572896 | tf_op jit(solution)/shard_map/while/body/eval_jaxpr/ppermute | solution.py:22
  738.0 28.8 %collective-permute-done.1 = f32[48,64,128]{2,1,0:T(8,128)S(1)} collective-permute-done((f32[48,64,128]{2,1,0:T(8,128)}, f32[48,64,128]{2,1,0:T(8,128)S(1)}, u32[]{:S(2)}, u32[]{:S(2)}) %collective-permute-start.1) | collective-permute-done | bytes 1572896 | tf_op jit(solution)/shard_map/while/body/eval_jaxpr/ppermute | solution.py:22
  770.9 28.8 %collective-permute-done.1 = f32[48,64,128]{2,1,0:T(8,128)S(1)} collective-permute-done((f32[48,64,128]{2,1,0:T(8,128)}, f32[48,64,128]{2,1,0:T(8,128)S(1)}, u32[]{:S(2)}, u32[]{:S(2)}) %collective-permute-start.1) | collective-permute-done | bytes 1572896 | tf_op jit(solution)/shard_map/while/body/eval_jaxpr/ppermute | solution.py:22
  799.7 6.0 multiply_reduce_fusion.5
  834.7 12.5 bitcast_add_fusion
  847.3 11.4 multiply_reduce_fusion.3
  862.9 4.2 pad_add_fusion
  879.1 17.5 %fusion.72 = f32[1536,6448]{0,1:T(8,128)} fusion(bf16[256,48]{0,1:T(8,128)(2,1)S(1)} %copy.182, bf16[256,3328]{0,1:T(8,128)(2,1)S(1)} %fusion.30, bf16[256,3072]{0,1:T(8,128)(2,1)} %get-tuple-element.395, bf16[1,256,1536]{2,1,0:T(8,128)(2,1)S(1)} %copy-done.15, f32[1536]{0:T(1024)S(1)} %copy-done.49, f32[256]{0:T(256)S(1)} %copy-done.74), kind=kOutput, calls=%fused_computation.116 | convolution fusion | flops 5082390528 | bytes 43711488 | tf_op jit(solution)/shard_map/dot_general | solution.py:59
  900.0 289.7 %reduce-scatter.11.cloned.1.call-done = f32[384,6448]{0,1:T(8,128)} async-done(((f32[1536,6448]{0,1:T(8,128)}), f32[384,6448]{0,1:T(8,128)}) %reduce-scatter.11.cloned.1.call-update) | async-done | bytes 9904144 | tf_op jit(solution)/shard_map/reduce_scatter | solution.py:228
  1189.7 10.7 copy.209
  1206.3 40.6 %all-reduce.26 = (f32[48]{0:T(128)}, f32[48]{0:T(128)}, f32[48]{0:T(128)}) all-reduce(f32[48]{0:T(128)S(1)} %add.197, f32[48]{0:T(128)S(1)} %add_multiply_fusion, f32[48]{0:T(128)S(1)} %reduce_sum.323), channel_id=1, replica_groups=mesh['dp'=4,'seq'=8] {'dp','seq'}, use_global_device_ids=true, to_apply=%region_40.42 | all-reduce | flops 144 | bytes 1152 | tf_op jit(solution)/shard_map/psum | solution.py:242
  1246.9 7.5 fusion.50
  1254.4 11.2 fusion.58
  1265.7 11.9 all-reduce.28
  1280.6 29.0 %all-reduce.27 = (f32[384]{0:T(512)S(1)}, f32[832,4]{0,1:T(4,128)S(1)}, f32[832]{0:T(1024)S(1)}, f32[768]{0:T(1024)S(1)}) all-reduce(f32[384]{0:T(512)S(1)} %dynamic-slice.24, f32[832,4]{0,1:T(4,128)S(1)} %copy.212, f32[832]{0:T(1024)S(1)} %dynamic-slice.30, f32[768]{0:T(1024)S(1)} %dynamic-slice.34), channel_id=3, replica_groups=mesh['dp'=4,'seq'=8] {'seq'}, use_global_device_ids=true, to_apply=%region_26.28.clone | all-reduce | flops 5312 | bytes 42496
  1312.0 10.0 reduce-scatter.15.cloned.1.call-done
  1322.1 177.1 %reduce-scatter.17.cloned.1.call-done = f32[48,6448]{1,0:T(8,128)} async-done(((f32[384,6448]{1,0:T(8,128)}), f32[48,6448]{1,0:T(8,128)}) %reduce-scatter.17.cloned.1.call-update) | async-done | bytes 1238032
  (342 shorter events, 159.9 us)
Async XLA Ops:
  7.2 137.9 %all-gather.4.cloned.1.call-start = ((), (), s32[]{:S(2)}) async-start(), calls=%async_computation.5 | async-start | bytes 20680704 | tf_op jit(solution)/shard_map/all_gather | solution.py:92
  7.9 504.1 %all-gather.6.cloned.1.call-start = ((), (), s32[]{:S(2)}) async-start(), calls=%async_computation.6 | async-start | bytes 9732096 | tf_op jit(solution)/shard_map/all_gather | solution.py:96
  8.7 890.7 %reduce-scatter.13.cloned.1.call-start = ((), (), s32[]{:S(2)}) async-start(), calls=%async_computation.8 | async-start | bytes 23592960 | tf_op jit(solution)/shard_map/reduce_scatter | solution.py:232
  9.4 116.7 %collective-permute-start.2 = (bf16[3]{0:T(256)(128)(2,1)S(1)}, bf16[3]{0:T(256)(128)(2,1)S(1)}, u32[]{:S(2)}, u32[]{:S(2)}) collective-permute-start(bf16[3]{0:T(256)(128)(2,1)S(1)} %convert_bitcast_fusion), channel_id=1, source_target_pairs={{0,1},{1,2},{2,3},{3,4},{4,5},{5,6},{6,7},{8,9},{9,10},{10,11},{11... | collective-permute-start | bytes 26 | tf_op jit(solution)/shard_map/ppermute | solution.py:22
  59.3 98.8 %copy-start.48 = (f32[1536]{0:T(1024)}, f32[1536]{0:T(1024)S(1)}, u32[]{:S(2)}) copy-start(f32[1536]{0:T(1024)S(1)} %convert_element_type.96) | copy-start | bytes 18436
  124.6 42.7 %copy-start.80 = (f32[48]{0:T(128)}, f32[48]{0:T(128)S(1)}, u32[]{:S(2)}) copy-start(f32[48]{0:T(128)S(1)} %exponential_negate_fusion) | copy-start | bytes 580
  124.6 33.6 %copy-start.73 = (f32[256]{0:T(256)}, f32[256]{0:T(256)S(1)}, u32[]{:S(2)}) copy-start(f32[256]{0:T(256)S(1)} %fusion.120) | copy-start | bytes 3076
  131.4 37.8 %copy-start.65 = (f32[256]{0:T(256)}, f32[256]{0:T(256)S(1)}, u32[]{:S(2)}) copy-start(f32[256]{0:T(256)S(1)} %get-tuple-element.409) | copy-start | bytes 3076
  131.4 35.9 %copy-start.67 = (f32[48]{0:T(128)S(1)}, f32[48]{0:T(128)}, u32[]{:S(2)}) copy-start(f32[48]{0:T(128)} %param.23) | copy-start | bytes 580
  163.4 15.8 %collective-permute-start.3 = (bf16[3,3328]{1,0:T(4,128)(2,1)}, bf16[3,3328]{1,0:T(4,128)(2,1)}, u32[]{:S(2)}, u32[]{:S(2)}) collective-permute-start(bf16[3,3328]{1,0:T(4,128)(2,1)} %copy.149), channel_id=1, source_target_pairs={{0,1},{1,2},{2,3},{3,4},{4,5},{5,6},{6,7},{8,9},{9,10},{10,11},{11... | collective-permute-start | bytes 59912 | tf_op jit(solution)/shard_map/ppermute | solution.py:22
  169.1 639.4 %copy-start.23 = (f32[48,2,128]{0,2,1:T(8,128)}, f32[48,2,128]{0,2,1:T(8,128)S(1)}, u32[]{:S(2)}) copy-start(f32[48,2,128]{0,2,1:T(8,128)S(1)} %copy.154) | copy-start | bytes 147460
  173.4 18.5 %copy-start.10 = (f32[256,3328]{0,1:T(8,128)}, f32[256,3328]{0,1:T(8,128)S(1)}, u32[]{:S(2)}) copy-start(f32[256,3328]{0,1:T(8,128)S(1)} %slice.131) | copy-start | bytes 10223620
  191.9 8.6 copy-start.5
  202.1 43.7 %collective-permute-start = (f32[48,64,128]{2,1,0:T(8,128)}, f32[48,64,128]{2,1,0:T(8,128)S(1)}, u32[]{:S(2)}, u32[]{:S(2)}) collective-permute-start(f32[48,64,128]{2,1,0:T(8,128)} %multiply_add_fusion.8), channel_id=1, source_target_pairs={{0,1},{1,2},{2,3},{3,4},{4,5},{5,6},{6,7},{8,9},{9,10},{10,11},{11... | collective-permute-start | bytes 4718600 | tf_op jit(solution)/shard_map/while/body/eval_jaxpr/ppermute | solution.py:22
  247.2 45.0 %collective-permute-start = (f32[48,64,128]{2,1,0:T(8,128)}, f32[48,64,128]{2,1,0:T(8,128)S(1)}, u32[]{:S(2)}, u32[]{:S(2)}) collective-permute-start(f32[48,64,128]{2,1,0:T(8,128)} %multiply_add_fusion.8), channel_id=1, source_target_pairs={{0,1},{1,2},{2,3},{3,4},{4,5},{5,6},{6,7},{8,9},{9,10},{10,11},{11... | collective-permute-start | bytes 4718600 | tf_op jit(solution)/shard_map/while/body/eval_jaxpr/ppermute | solution.py:22
  293.5 37.3 %collective-permute-start = (f32[48,64,128]{2,1,0:T(8,128)}, f32[48,64,128]{2,1,0:T(8,128)S(1)}, u32[]{:S(2)}, u32[]{:S(2)}) collective-permute-start(f32[48,64,128]{2,1,0:T(8,128)} %multiply_add_fusion.8), channel_id=1, source_target_pairs={{0,1},{1,2},{2,3},{3,4},{4,5},{5,6},{6,7},{8,9},{9,10},{10,11},{11... | collective-permute-start | bytes 4718600 | tf_op jit(solution)/shard_map/while/body/eval_jaxpr/ppermute | solution.py:22
  332.1 36.4 %collective-permute-start = (f32[48,64,128]{2,1,0:T(8,128)}, f32[48,64,128]{2,1,0:T(8,128)S(1)}, u32[]{:S(2)}, u32[]{:S(2)}) collective-permute-start(f32[48,64,128]{2,1,0:T(8,128)} %multiply_add_fusion.8), channel_id=1, source_target_pairs={{0,1},{1,2},{2,3},{3,4},{4,5},{5,6},{6,7},{8,9},{9,10},{10,11},{11... | collective-permute-start | bytes 4718600 | tf_op jit(solution)/shard_map/while/body/eval_jaxpr/ppermute | solution.py:22
  369.8 35.4 %collective-permute-start = (f32[48,64,128]{2,1,0:T(8,128)}, f32[48,64,128]{2,1,0:T(8,128)S(1)}, u32[]{:S(2)}, u32[]{:S(2)}) collective-permute-start(f32[48,64,128]{2,1,0:T(8,128)} %multiply_add_fusion.8), channel_id=1, source_target_pairs={{0,1},{1,2},{2,3},{3,4},{4,5},{5,6},{6,7},{8,9},{9,10},{10,11},{11... | collective-permute-start | bytes 4718600 | tf_op jit(solution)/shard_map/while/body/eval_jaxpr/ppermute | solution.py:22
  406.6 34.5 %collective-permute-start = (f32[48,64,128]{2,1,0:T(8,128)}, f32[48,64,128]{2,1,0:T(8,128)S(1)}, u32[]{:S(2)}, u32[]{:S(2)}) collective-permute-start(f32[48,64,128]{2,1,0:T(8,128)} %multiply_add_fusion.8), channel_id=1, source_target_pairs={{0,1},{1,2},{2,3},{3,4},{4,5},{5,6},{6,7},{8,9},{9,10},{10,11},{11... | collective-permute-start | bytes 4718600 | tf_op jit(solution)/shard_map/while/body/eval_jaxpr/ppermute | solution.py:22
  442.5 33.6 %collective-permute-start = (f32[48,64,128]{2,1,0:T(8,128)}, f32[48,64,128]{2,1,0:T(8,128)S(1)}, u32[]{:S(2)}, u32[]{:S(2)}) collective-permute-start(f32[48,64,128]{2,1,0:T(8,128)} %multiply_add_fusion.8), channel_id=1, source_target_pairs={{0,1},{1,2},{2,3},{3,4},{4,5},{5,6},{6,7},{8,9},{9,10},{10,11},{11... | collective-permute-start | bytes 4718600 | tf_op jit(solution)/shard_map/while/body/eval_jaxpr/ppermute | solution.py:22
  479.9 17.4 %copy-start.18 = (f32[256,48,64]{0,2,1:T(8,128)}, f32[256,48,64]{0,2,1:T(8,128)S(1)}, u32[]{:S(2)}) copy-start(f32[256,48,64]{0,2,1:T(8,128)S(1)} %fusion.105) | copy-start | bytes 9437188
  501.4 19.1 %copy-start.63 = (f32[256]{0:T(256)}, f32[256]{0:T(256)S(1)}, u32[]{:S(2)}) copy-start(f32[256]{0:T(256)S(1)} %fusion.121) | copy-start | bytes 3076
  511.2 678.4 %reduce-scatter.11.cloned.1.call-start = ((), (), s32[]{:S(2)}) async-start(), calls=%async_computation.7 | async-start | bytes 49520640 | tf_op jit(solution)/shard_map/reduce_scatter | solution.py:228
  566.7 33.2 %collective-permute-start.1 = (f32[48,64,128]{2,1,0:T(8,128)}, f32[48,64,128]{2,1,0:T(8,128)S(1)}, u32[]{:S(2)}, u32[]{:S(2)}) collective-permute-start(f32[48,64,128]{2,1,0:T(8,128)} %multiply_add_fusion.9), channel_id=1, source_target_pairs={{1,0},{2,1},{3,2},{4,3},{5,4},{6,5},{7,6},{9,8},{10,9},{11,10},{12... | collective-permute-start | bytes 4718600 | tf_op jit(solution)/shard_map/while/body/eval_jaxpr/ppermute | solution.py:22
  602.7 32.1 %collective-permute-start.1 = (f32[48,64,128]{2,1,0:T(8,128)}, f32[48,64,128]{2,1,0:T(8,128)S(1)}, u32[]{:S(2)}, u32[]{:S(2)}) collective-permute-start(f32[48,64,128]{2,1,0:T(8,128)} %multiply_add_fusion.9), channel_id=1, source_target_pairs={{1,0},{2,1},{3,2},{4,3},{5,4},{6,5},{7,6},{9,8},{10,9},{11,10},{12... | collective-permute-start | bytes 4718600 | tf_op jit(solution)/shard_map/while/body/eval_jaxpr/ppermute | solution.py:22
  637.6 30.6 %collective-permute-start.1 = (f32[48,64,128]{2,1,0:T(8,128)}, f32[48,64,128]{2,1,0:T(8,128)S(1)}, u32[]{:S(2)}, u32[]{:S(2)}) collective-permute-start(f32[48,64,128]{2,1,0:T(8,128)} %multiply_add_fusion.9), channel_id=1, source_target_pairs={{1,0},{2,1},{3,2},{4,3},{5,4},{6,5},{7,6},{9,8},{10,9},{11,10},{12... | collective-permute-start | bytes 4718600 | tf_op jit(solution)/shard_map/while/body/eval_jaxpr/ppermute | solution.py:22
  671.0 30.1 %collective-permute-start.1 = (f32[48,64,128]{2,1,0:T(8,128)}, f32[48,64,128]{2,1,0:T(8,128)S(1)}, u32[]{:S(2)}, u32[]{:S(2)}) collective-permute-start(f32[48,64,128]{2,1,0:T(8,128)} %multiply_add_fusion.9), channel_id=1, source_target_pairs={{1,0},{2,1},{3,2},{4,3},{5,4},{6,5},{7,6},{9,8},{10,9},{11,10},{12... | collective-permute-start | bytes 4718600 | tf_op jit(solution)/shard_map/while/body/eval_jaxpr/ppermute | solution.py:22
  703.9 30.1 %collective-permute-start.1 = (f32[48,64,128]{2,1,0:T(8,128)}, f32[48,64,128]{2,1,0:T(8,128)S(1)}, u32[]{:S(2)}, u32[]{:S(2)}) collective-permute-start(f32[48,64,128]{2,1,0:T(8,128)} %multiply_add_fusion.9), channel_id=1, source_target_pairs={{1,0},{2,1},{3,2},{4,3},{5,4},{6,5},{7,6},{9,8},{10,9},{11,10},{12... | collective-permute-start | bytes 4718600 | tf_op jit(solution)/shard_map/while/body/eval_jaxpr/ppermute | solution.py:22
  736.8 30.1 %collective-permute-start.1 = (f32[48,64,128]{2,1,0:T(8,128)}, f32[48,64,128]{2,1,0:T(8,128)S(1)}, u32[]{:S(2)}, u32[]{:S(2)}) collective-permute-start(f32[48,64,128]{2,1,0:T(8,128)} %multiply_add_fusion.9), channel_id=1, source_target_pairs={{1,0},{2,1},{3,2},{4,3},{5,4},{6,5},{7,6},{9,8},{10,9},{11,10},{12... | collective-permute-start | bytes 4718600 | tf_op jit(solution)/shard_map/while/body/eval_jaxpr/ppermute | solution.py:22
  769.6 30.1 %collective-permute-start.1 = (f32[48,64,128]{2,1,0:T(8,128)}, f32[48,64,128]{2,1,0:T(8,128)S(1)}, u32[]{:S(2)}, u32[]{:S(2)}) collective-permute-start(f32[48,64,128]{2,1,0:T(8,128)} %multiply_add_fusion.9), channel_id=1, source_target_pairs={{1,0},{2,1},{3,2},{4,3},{5,4},{6,5},{7,6},{9,8},{10,9},{11,10},{12... | collective-permute-start | bytes 4718600 | tf_op jit(solution)/shard_map/while/body/eval_jaxpr/ppermute | solution.py:22
  806.6 13.5 copy-start.31
  834.7 12.6 copy-start.11
  834.7 12.6 copy-start.14
  834.7 12.6 copy-start.75
  834.7 12.6 copy-start.76
  834.7 12.6 copy-start.77
  869.9 5.2 collective-permute-start.4
  879.1 17.5 %copy-start.22 = (bf16[256,3328]{0,1:T(8,128)(2,1)}, bf16[256,3328]{0,1:T(8,128)(2,1)S(1)}, u32[]{:S(2)}) copy-start(bf16[256,3328]{0,1:T(8,128)(2,1)S(1)} %fusion.30) | copy-start | bytes 5111812
  896.7 382.8 %reduce-scatter.19.cloned.1.call-start = ((), (), s32[]{:S(2)}) async-start(), calls=%async_computation.11 | async-start | bytes 2129920
  899.3 422.7 %reduce-scatter.15.cloned.1.call-start = ((), (), s32[]{:S(2)}) async-start(), calls=%async_computation.9 | async-start | bytes 5308416 | tf_op jit(solution)/shard_map/reduce_scatter | solution.py:240
  899.9 599.3 %reduce-scatter.17.cloned.1.call-start = ((), (), s32[]{:S(2)}) async-start(), calls=%async_computation.10 | async-start | bytes 11280384
  1200.4 46.5 %copy-start.4 = (f32[256,3072]{0,1:T(8,128)S(1)}, f32[256,3072]{0,1:T(8,128)}, u32[]{:S(2)}) copy-start(f32[256,3072]{0,1:T(8,128)} %copy-done.2) | copy-start | bytes 9437188
  1200.4 46.5 %copy-start.64 = (f32[256]{0:T(256)S(1)}, f32[256]{0:T(256)}, u32[]{:S(2)}) copy-start(f32[256]{0:T(256)} %copy-done.63) | copy-start | bytes 3076
  1254.4 11.2 copy-start.52
  1254.4 11.3 copy-start.70
  1254.4 23.4 %copy-start.72 = (f32[256]{0:T(256)S(1)}, f32[256]{0:T(256)}, u32[]{:S(2)}) copy-start(f32[256]{0:T(256)} %copy-done.71) | copy-start | bytes 3076
  1254.4 23.4 %copy-start.16 = (bf16[1,256,1536]{2,1,0:T(8,128)(2,1)S(1)}, bf16[1,256,1536]{2,1,0:T(8,128)(2,1)}, u32[]{:S(2)}) copy-start(bf16[1,256,1536]{2,1,0:T(8,128)(2,1)} %param.17) | copy-start | bytes 2359300
  1254.4 23.4 %copy-start.29 = (bf16[1,256,1536]{2,1,0:T(8,128)(2,1)S(1)}, bf16[1,256,1536]{2,1,0:T(8,128)(2,1)}, u32[]{:S(2)}) copy-start(bf16[1,256,1536]{2,1,0:T(8,128)(2,1)} %param.28) | copy-start | bytes 2359300
  (66 other events, 312.8 us)
Sparse Core Ops, SparseCore 0:
  10.9 134.1 all-gather.3
  148.0 88.0 all-gather.5
  511.3 150.2 reduce-scatter.12
  896.8 292.8 reduce-scatter.10
  1192.1 29.5 reduce-scatter.18
  1226.2 95.7 reduce-scatter.14
  1326.7 172.4 reduce-scatter.16
where the time goes:
time: 1510 us
  waiting for transfers between devices  931 us (62%)
  blocking collectives  185 us (12%)
  matrix products  158 us (10%)
  other arithmetic  99.4 us (7%)
  starting transfers between devices  56.4 us (4%)
  local copies, waits for them, and re-layouts  55.2 us (4%)
  between operations  21.1 us (1%)
    ppermute x17, waiting for transfers between devices, passed_along(): return lax.ppermute(block, axis, route)  438 us
    reduce_scatter x1, waiting for transfers between devices, body(): lax.psum_scatter(grad_parts[1], 'dp', scatter_dimension=0, tiled=True)  290 us
    unnamed x9, waiting for transfers between devices  179 us
    unnamed x3, blocking collectives  83.1 us
    all_gather x1, blocking collectives, body(): lax.all_gather(shards[2], ('dp', 'seq'), axis=0, tiled=True)  61.7 us
    ppermute x17, starting transfers between devices, passed_along(): return lax.ppermute(block, axis, route)  56.1 us
    dot_general x3, matrix products, group_math(): inside = jnp.einsum('tsh,shp->thp', mixing, heads_x, precision=HIGHEST)  53 us
    psum x1, blocking collectives, body(): lax.psum((shift_one + shift_two, rate_one + rate_two, skip_grad), ('dp',...  40.6 us
  transfers between devices with their start and end apart: 24, of which 19 were waited for; matrix products, arithmetic and copies ran while one was open for 20% of the time, Pallas kernels for 0%

commit v1 on v0

--- a/solution.py
+++ b/solution.py
@@ -1,6 +1,11 @@
+import functools
+
 import jax
 import jax.numpy as jnp
 from jax import lax
+from jax.experimental import pallas as pl
+from jax.experimental.pallas import tpu as pltpu
+from jax.sharding import Mesh
 from jax.sharding import PartitionSpec as P
 
 HEADS = 48
@@ -67,7 +72,7 @@
     )
 
 
-def body(
+def whole_body(
     tokens,
     segment_ids,
     pre_gain,
@@ -254,37 +259,518 @@
         sums[5],
     )
 
+AXES = ("dpo", "dpi", "so", "si")
+MESH = pl.DeviceIdType.MESH
+XCOLS = INNER // 4
+CCOLS = XCOLS + 2 * STATE + 128
+VMEM = pl.BlockSpec(memory_space=pltpu.VMEM)
+
+
+class Wires:
+    def __init__(self, send, recv):
+        self.send, self.recv, self.used, self.pending = send, recv, 0, []
+
+    def slot(self):
+        self.used += 1
+        return self.used - 1
+
+    def copy(self, src, dst, slot, device):
+        return pltpu.make_async_remote_copy(
+            src_ref=src, dst_ref=dst, send_sem=self.send.at[slot], recv_sem=self.recv.at[slot],
+            device_id=device, device_id_type=MESH,
+        )
+
+    def start(self, src, dst, slot, device, when=None):
+        copy = self.copy(src, dst, slot, device)
+        guarded(when, copy.start)
+        self.pending.append((copy, when))
+
+    def arrived(self, landing, slot, device, when=None):
+        guarded(when, self.copy(landing, landing, slot, device).wait_recv)
+
+    def finish(self):
+        for copy, when in self.pending:
+            guarded(when, copy.wait_send)
+        self.pending = []
+
+
+def guarded(when, action):
+    if when is None:
+        action()
+    else:
+        pl.when(when)(action)
+
+
+def greet(here, size):
+    a, c, b, s = here
+    barrier = pltpu.get_barrier_semaphore()
+    met = 0
+    for rel in range(1, 4):
+        pl.semaphore_signal(barrier, inc=1, device_id=member(here, rel), device_id_type=MESH)
+        met = met + 1
+    for k in range(1, size["so"]):
+        pl.semaphore_signal(
+            barrier, inc=1, device_id=(a, c, lax.rem(b + k, size["so"]), s), device_id_type=MESH
+        )
+        met = met + 1
+    for k in range(1, size["dpo"]):
+        pl.semaphore_signal(
+            barrier, inc=1, device_id=(lax.rem(a + k, size["dpo"]), c, b, s), device_id_type=MESH
+        )
+        met = met + 1
+    pl.semaphore_wait(barrier, met)
+
+
+def member(here, rel):
+    a, c, b, s = here
+    return (a, c ^ (rel >> 1), b, s ^ (rel & 1))
+
+
+def place():
+    return tuple(lax.axis_index(name) for name in AXES)
+
+
+def gather_kernel(size, wc_in, wg_in, wo_in, tok, cot, wc, wg, wo, toks, cots, send, recv, local):
+    here = place()
+    a, c, b, s = here
+    n, nx = size["so"], size["dpo"]
+    wires = Wires(send, recv)
+    mine = 2 * c + s
+    own = []
+
+    def keep(src, dst, when=None):
+        copy = pltpu.make_async_copy(src, dst, local.at[len(own)])
+        guarded(when, copy.start)
+        own.append((copy, when))
+
+    greet(here, size)
+    rows = wc_in.shape[1]
+    span = 2 * rows
+    shard = lambda w, cc, ss: w.at[a, cc, pl.ds(pl.multiple_of(span * b + rows * ss, 16), rows)]
+    unit = lambda w, aa, bb: w.at[aa, :, pl.ds(pl.multiple_of(span * bb, 16), span)]
+    halves = wo_in.shape[0]
+    wo_half = lambda aa, bb, ss: wo.at[aa, bb // 2, pl.ds(pl.multiple_of(halves * ss, 16), halves)]
+    holder = lax.rem(b, 2) == s
+    first = {}
+    for name, src, dst in (("c", wc_in, wc), ("g", wg_in, wg)):
+        keep(src.at[mine], shard(dst, c, s))
+        for rel in range(1, 4):
+            _, cc, _, ss = member(here, rel)
+            first[name, rel] = wires.slot()
+            wires.start(src.at[2 * cc + ss], shard(dst, c, s), first[name, rel], member(here, rel))
+        if name == "c":
+            for key, src2, dst2 in (("t", tok, toks), ("k", cot, cots)):
+                keep(src2, dst2.at[mine])
+                for rel in range(1, 4):
+                    first[key, rel] = wires.slot()
+                    wires.start(src2, dst2.at[mine], first[key, rel], member(here, rel))
+    keep(wo_in, wo_half(a, b, s), holder)
+    first["o"] = wires.slot()
+    wires.start(wo_in, wo_half(a, b, s), first["o"], member(here, 1), jnp.logical_not(holder))
+    for copy, when in own:
+        guarded(when, copy.wait)
+
+    def spread(get, has):
+        def cross(bb, when, slots):
+            for k in range(1, nx):
+                wires.start(get(a, bb), get(a, bb), slots[k], (lax.rem(a + k, nx), c, b, s), when)
+        crossing = {}
+        def note(bb, when):
+            slots = {k: wires.slot() for k in range(1, nx)}
+            cross(bb, when, slots)
+            crossing[len(crossing)] = (bb, when, slots)
+        up = {j: wires.slot() for j in range(1, n)}
+        down = {j: wires.slot() for j in range(1, n)}
+        above, below = (a, c, jnp.minimum(b + 1, n - 1), s), (a, c, jnp.maximum(b - 1, 0), s)
+        wires.start(get(a, b), get(a, b), up[1], above, (b + 1 < n) & has(b))
+        wires.start(get(a, b), get(a, b), down[1], below, (b > 0) & has(b))
+        note(b, has(b))
+        for j in range(1, n):
+            for slots, origin, there, target, onward in (
+                (up, jnp.maximum(b - j, 0), (b - j >= 0) & has(b + j), above, b + 1 < n),
+                (down, jnp.minimum(b + j, n - 1), (b + j < n) & has(b + j), below, b > 0),
+            ):
+                wires.arrived(get(a, origin), slots[j], below, there)
+                if j + 1 < n:
+                    wires.start(get(a, origin), get(a, origin), slots[j + 1], target, there & onward)
+                note(origin, there)
+        return crossing
+
+    def settle(get, crossing):
+        for bb, when, slots in crossing.values():
+            for k in range(1, nx):
+                aa = lax.rem(a + nx - k, nx)
+                wires.arrived(get(aa, bb), slots[k], (aa, c, b, s), when)
+
+    always = lambda bb: jnp.bool_(True)
+    crossings = []
+    for name, w in (("c", wc), ("g", wg)):
+        for rel in range(1, 4):
+            _, cc, _, ss = member(here, rel)
+            wires.arrived(shard(w, cc, ss), first[name, rel], member(here, rel))
+        get = lambda aa, bb, w=w: unit(w, aa, bb)
+        crossings.append((get, spread(get, always)))
+    wires.arrived(wo_half(a, b, 1 - s), first["o"], member(here, 1), holder)
+    get = lambda aa, bb: wo.at[aa, bb // 2]
+    crossings.append((get, spread(get, lambda bb: lax.rem(bb, 2) == s)))
+    for key, dst in (("t", toks), ("k", cots)):
+        for rel in range(1, 4):
+            _, cc, _, ss = member(here, rel)
+            wires.arrived(dst.at[2 * cc + ss], first[key, rel], member(here, rel))
+    for get, crossing in crossings:
+        settle(get, crossing)
+    wires.finish()
+
+
+def gather(size, wc_in, wg_in, wo_in, tok, cot):
+    rows = size["so"] * 2 * wc_in.shape[1]
+    lead = (size["dpo"], 2, rows)
+    shapes = (
+        jax.ShapeDtypeStruct(lead + (wc_in.shape[2],), jnp.bfloat16),
+        jax.ShapeDtypeStruct(lead + (wg_in.shape[2],), jnp.bfloat16),
+        jax.ShapeDtypeStruct((size["dpo"], size["so"] // 2, 2 * wo_in.shape[0], wo_in.shape[1]), jnp.bfloat16),
+        jax.ShapeDtypeStruct((4,) + tok.shape, jnp.bfloat16),
+        jax.ShapeDtypeStruct((4,) + cot.shape, jnp.bfloat16),
+    )
+    slots = 13 + 3 * (2 * (size["so"] - 1) + (size["dpo"] - 1) * (2 * size["so"] - 1))
+    return pl.pallas_call(
+        functools.partial(gather_kernel, size),
+        out_shape=shapes,
+        in_specs=[pl.BlockSpec(memory_space=pl.ANY)] * 5,
+        out_specs=[pl.BlockSpec(memory_space=pl.ANY)] * 5,
+        scratch_shapes=[
+            pltpu.SemaphoreType.DMA((slots,)),
+            pltpu.SemaphoreType.DMA((slots,)),
+            pltpu.SemaphoreType.DMA((5,)),
+        ],
+        compiler_params=pltpu.CompilerParams(collective_id=1, has_side_effects=True),
+    )(wc_in, wg_in, wo_in, tok, cot)
+
+
+def reduce_kernel(size, gc, gg, go, oc, og, oo, xc, xg, xo, zc, zg, zo, send, recv):
+    here = place()
+    a, c, b, s = here
+    n, nx = size["so"], size["dpo"]
+    wires = Wires(send, recv)
+    greet(here, size)
+    span = gc.shape[2] // n
+    rows = span // 2
+    halves = go.shape[2] // 2
+    block = lambda bb: pl.ds(pl.multiple_of(span * bb, 16), span)
+    always = lambda bb: None
+    odd = lambda bb: lax.rem(bb, 2) == s
+    parts = (
+        (gc, xc, zc, lambda g, aa, bb: g.at[aa, :, block(bb)], always),
+        (gg, xg, zg, lambda g, aa, bb: g.at[aa, :, block(bb)], always),
+        (go, xo, zo, lambda g, aa, bb: g.at[aa, bb // 2], odd),
+    )
+    order = [k for k in range(1, n)] + [0]
+    flown = {}
+    for p, (g, x, z, get, has) in enumerate(parts):
+        for k in order:
+            bb = lax.rem(b + k, n)
+            for h in range(1, nx):
+                aa = lax.rem(a + h, nx)
+                flown[p, k, h] = wires.slot()
+                wires.start(get(g, aa, bb), x.at[h - 1, k], flown[p, k, h], (aa, c, b, s), has(bb))
+    hops = {}
+    for p, (g, x, z, get, has) in enumerate(parts):
+        for k in order:
+            bb = lax.rem(b + k, n)
+            for h in range(1, nx):
+                wires.arrived(x.at[h - 1, k], flown[p, k, h], (lax.rem(a + nx - h, nx), c, b, s), has(bb))
+
+            def add():
+                total = get(g, a, bb)[...].astype(jnp.float32)
+                for h in range(1, nx):
+                    total = total + x[h - 1, k].astype(jnp.float32)
+                x[0, k] = total.astype(jnp.bfloat16)
+
+            guarded(has(bb), add)
+            if k > 0:
+                hops[p, k] = wires.slot()
+                wires.start(x.at[0, k], z.at[k - 1], hops[p, k], (a, c, bb, s), has(bb))
+    back = {}
+    for p, (g, x, z, get, has) in enumerate(parts):
+        for k in range(1, n):
+            wires.arrived(z.at[k - 1], hops[p, k], (a, c, lax.rem(b + n - k, n), s), has(b))
+
+        def total():
+            t = x[0, 0].astype(jnp.float32)
+            for k in range(1, n):
+                t = t + z[k - 1].astype(jnp.float32)
+            return t
+
+        if p < 2:
+            out = (oc, og)[p]
+            t = total().astype(jnp.bfloat16)
+            z[0] = t
+            mine = 2 * c + s
+            out[mine] = z[0, c, pl.ds(pl.multiple_of(rows * s, 16), rows)]
+            for rel in range(1, 4):
+                _, cc, _, ss = member(here, rel)
+                back[p, rel] = wires.slot()
+                wires.start(
+                    z.at[0, cc, pl.ds(pl.multiple_of(rows * ss, 16), rows)], out.at[mine],
+                    back[p, rel], member(here, rel),
+                )
+        else:
+            def close():
+                z[0] = total().astype(jnp.bfloat16)
+                oo[...] = z[0, pl.ds(pl.multiple_of(halves * s, 16), halves)]
+            guarded(odd(b), close)
+            back[p] = wires.slot()
+            wires.start(
+                z.at[0, pl.ds(pl.multiple_of(halves * (1 - s), 16), halves)], oo, back[p], member(here, 1), odd(b)
+            )
+    for p, out in ((0, oc), (1, og)):
+        for rel in range(1, 4):
+            _, cc, _, ss = member(here, rel)
+            wires.arrived(out.at[2 * cc + ss], back[p, rel], member(here, rel))
+    wires.arrived(oo, back[2], member(here, 1), jnp.logical_not(odd(b)))
+    wires.finish()
+
+
+def reduce(size, gc, gg, go):
+    n, nx = size["so"], size["dpo"]
+    span = gc.shape[2] // n
+    rows = span // 2
+    outs = (
+        jax.ShapeDtypeStruct((4, rows, gc.shape[3]), jnp.bfloat16),
+        jax.ShapeDtypeStruct((4, rows, gg.shape[3]), jnp.bfloat16),
+        jax.ShapeDtypeStruct((go.shape[2] // 2, go.shape[3]), jnp.bfloat16),
+    )
+    units = [(2, span, gc.shape[3]), (2, span, gg.shape[3]), go.shape[2:]]
+    slots = 3 * n * (nx - 1) + 3 * (n - 1) + 7
+    return pl.pallas_call(
+        functools.partial(reduce_kernel, size),
+        out_shape=outs,
+        in_specs=[VMEM] * 3,
+        out_specs=[VMEM] * 3,
+        scratch_shapes=[pltpu.VMEM((nx - 1, n) + tuple(u), jnp.bfloat16) for u in units]
+        + [pltpu.VMEM((n - 1,) + tuple(u), jnp.bfloat16) for u in units]
+        + [pltpu.SemaphoreType.DMA((slots,)), pltpu.SemaphoreType.DMA((slots,))],
+        compiler_params=pltpu.CompilerParams(
+            collective_id=2, has_side_effects=True, vmem_limit_bytes=56 * 2**20
+        ),
+    )(gc, gg, go)
+
+
+def split_classes(full, size):
+    lead = full.shape[:-1]
+    w = full.shape[-1] // (size["dpo"] * 2 * size["so"])
+    cut = full.reshape(lead + (size["dpo"], 2, size["so"] // 2, 2, w))
+    k = len(lead)
+    order = (k + 1, k + 3) + tuple(range(k)) + (k, k + 2, k + 4)
+    return cut.transpose(order).reshape((2, 2) + lead + (full.shape[-1] // 4,))
+
+
+def join_classes(parts, size):
+    lead = parts.shape[2:-1]
+    w = parts.shape[-1] // (size["dpo"] * size["so"] // 2)
+    k = len(lead)
+    cut = parts.reshape((2, 2) + lead + (size["dpo"], size["so"] // 2, w))
+    order = tuple(range(2, 2 + k)) + (2 + k, 0, 3 + k, 1, 4 + k)
+    return cut.transpose(order).reshape(lead + (parts.shape[-1] * 4,))
+
+
+def fast_body(size, tokens, segment_ids, pre_gain, in_weight, conv_weight, conv_bias, dt_bias, a_log, skip_gain, norm_gain, out_weight, cotangent):
+    here = place()
+    a, c, b, s = here
+    group = ("dpi", "si")
+    hl = HEADS // 4
+    margin = CONVW - 1
+    tok, cot, doc = tokens[0], cotangent[0], segment_ids[0]
+    own = doc.shape[0]
+    rows = in_weight.shape[0]
+    wg_in = split_classes(in_weight[:, :INNER], size).reshape(4, rows, XCOLS)
+    wx_in = split_classes(in_weight[:, INNER : 2 * INNER], size).reshape(4, rows, XCOLS)
+    bc_in = jnp.broadcast_to(in_weight[None, :, 2 * INNER : INNER + XBC], (4, rows, 2 * STATE))
+    dt_in = split_classes(in_weight[:, INNER + XBC :], size).reshape(4, rows, hl)
+    wc_in = jnp.concatenate([wx_in, bc_in, dt_in, jnp.zeros((4, rows, 128 - hl), jnp.bfloat16)], axis=2)
+    wc, wg, wo, toks, cots = gather(size, wc_in, wg_in, out_weight, tok, cot)
+    wc = wc.reshape(-1, CCOLS)
+    wg = wg.reshape(-1, XCOLS)
+    wo = wo.reshape(-1, wo.shape[-1])
+    everywhere = lambda v: lax.all_gather(v, AXES, axis=0, tiled=True)
+    pick = lambda v: lax.dynamic_index_in_dim(
+        lax.dynamic_index_in_dim(split_classes(v, size), c, 0, False), s, 0, False
+    )
+    gain1 = everywhere(pre_gain).astype(jnp.float32)
+    gain2 = pick(everywhere(norm_gain).astype(jnp.float32))
+    kern = everywhere(conv_weight).astype(jnp.float32).T
+    kern = jnp.concatenate([pick(kern[:, :INNER]), kern[:, INNER:]], axis=1)
+    bias = everywhere(conv_bias).astype(jnp.float32)
+    bias = jnp.concatenate([pick(bias[:INNER]), bias[INNER:]])
+    shift, rate, skip = pick(dt_bias), pick(a_log), pick(skip_gain)
+    docs = lax.all_gather(doc, group, axis=0).reshape(2, 2 * own)
+    n = size["so"]
+    up = [(i, i + 1) for i in range(n - 1)]
+    down = [(i + 1, i) for i in range(n - 1)]
+    toks = toks.reshape(2, 2 * own, -1)
+    cots = cots.reshape(2, 2 * own, -1)
+    halo = lax.ppermute(toks[:, 2 * own - margin :], "so", up)
+    halo_ids = jnp.where(b > 0, lax.ppermute(docs[:, 2 * own - margin :], "so", up), -1)
+    rowsx = jnp.concatenate([halo, toks], axis=1).astype(jnp.float32)
+    ext_ids = jnp.concatenate([halo_ids, docs], axis=1)
+    normed, _ = jax.vjp(rms_scale, rowsx, gain1)
+    normed_low = normed.astype(jnp.bfloat16)
+    projected = jnp.einsum("qtd,dk->qtk", normed_low, wc, preferred_element_type=jnp.float32)
+    gate_z = jnp.einsum("qtd,dk->qtk", normed_low[:, margin:], wg, preferred_element_type=jnp.float32)
+    length = 2 * own
+    count = length // GROUP
+    dt_raw = projected[:, margin:, XCOLS + 2 * STATE : XCOLS + 2 * STATE + hl]
+
+    def convolve(extended, kernel, offset_bias):
+        def one(ext, ids):
+            total = offset_bias
+            for offset in range(CONVW):
+                linked = (ids[offset : offset + length] == ids[margin:])[:, None]
+                total = total + jnp.where(linked, ext[offset : offset + length], 0.0) * kernel[offset]
+            return jax.nn.silu(total)
+        return jax.vmap(one)(extended, ext_ids)
+
+    activated, conv_back = jax.vjp(convolve, projected[:, :, : XCOLS + 2 * STATE], kern, bias)
+
+    def zero_state(acts_in, raw_in, shift_in, rate_in):
+        def one(acts, raw, doc_ids, prior_id):
+            heads_x = acts[:, :XCOLS].reshape(length, hl, HEADDIM)
+            b_rows = acts[:, XCOLS : XCOLS + STATE]
+            c_rows = acts[:, XCOLS + STATE :]
+            steps_dt = jax.nn.softplus(raw + shift_in)
+            log_decay = -jnp.exp(rate_in) * steps_dt
+            befores = jnp.concatenate([prior_id[None], doc_ids.reshape(count, GROUP)[:-1, GROUP - 1]])
+            items = (
+                befores,
+                heads_x.reshape(count, GROUP, hl, HEADDIM),
+                b_rows.reshape(count, GROUP, STATE),
+                c_rows.reshape(count, GROUP, STATE),
+                steps_dt.reshape(count, GROUP, hl),
+                log_decay.reshape(count, GROUP, hl),
+                doc_ids.reshape(count, GROUP),
+            )
+            final = jnp.zeros((hl, HEADDIM, STATE), jnp.float32)
+            outs = []
+            for i in range(count):
+                out, final = group_math(final, *[v[i] for v in items])
+                outs.append(out)
+            factor = jnp.exp(jnp.sum(log_decay, axis=0)) * (doc_ids[length - 1] == prior_id)
+            return (jnp.stack(outs).reshape(length, hl, HEADDIM), factor, final)
+        return jax.vmap(one)(acts_in, raw_in, docs, ext_ids[:, margin - 1])
+
+    def incoming(acts_in, raw_in, shift_in, rate_in, start_state):
+        def one(acts, raw, doc_ids, prior_id, state):
+            steps_dt = jax.nn.softplus(raw + shift_in)
+            running = jnp.cumsum(-jnp.exp(rate_in) * steps_dt, axis=0)
+            factor = jnp.exp(running) * (doc_ids == prior_id)[:, None]
+            return jnp.einsum("tn,hpn->thp", acts[:, XCOLS + STATE :], state, precision=HIGHEST) * factor[:, :, None]
+        return jax.vmap(one)(acts_in, raw_in, docs, ext_ids[:, margin - 1], start_state)
+
+    (local_y, factor, local_state), zero_back = jax.vjp(zero_state, activated, dt_raw, shift, rate)
+    all_states = lax.all_gather(local_state, "so", axis=0)
+    all_factors = lax.all_gather(factor, "so", axis=0)
+    start_state = jnp.zeros_like(local_state)
+    for i in range(n - 1):
+        step = all_factors[i][:, :, None, None] * start_state + all_states[i]
+        start_state = jnp.where(i < b, step, start_state)
+    carried_y, in_back = jax.vjp(incoming, activated, dt_raw, shift, rate, start_state)
+    heads_x = activated[:, :, :XCOLS].reshape(2, length, hl, HEADDIM)
+    mixer_out = (local_y + carried_y + skip[:, None] * heads_x).reshape(2, length, XCOLS)
+
+    grad_gated = jnp.einsum("qtd,kd->qtk", cots, wo, preferred_element_type=jnp.float32)
+    silu_z, silu_back = jax.vjp(jax.nn.silu, gate_z)
+    v = mixer_out * silu_z
+    u = grad_gated * gain2
+    sums = lax.psum(jnp.stack([jnp.sum(v * v, axis=-1), jnp.sum(u * v, axis=-1)]), group)
+    r = lax.rsqrt(sums[0] / INNER + EPSILON)[:, :, None]
+    mean_uv = sums[1][:, :, None] / INNER
+    gated_low = (v * r * gain2).astype(jnp.bfloat16)
+    grad_v = r * u - r * r * r * v * mean_uv
+    norm_gain_grad = jnp.sum(grad_gated * v * r, axis=(0, 1))
+    grad_mixer = grad_v * silu_z
+    (grad_gate_z,) = silu_back(grad_v * mixer_out)
+    branch = jnp.einsum("qtk,kd->qtd", gated_low, wo, preferred_element_type=jnp.float32)
+    out_weight_grad = jnp.einsum("qtk,qtd->kd", gated_low, cots, preferred_element_type=jnp.float32)
+    branch = lax.psum_scatter(branch.reshape(4, own, -1), group, scatter_dimension=0, tiled=False)
+    mixed = (tok.astype(jnp.float32) + branch).astype(jnp.bfloat16)
+
+    grad_heads = grad_mixer.reshape(2, length, hl, HEADDIM)
+    skip_grad = jnp.sum(grad_heads * heads_x, axis=(0, 1, 3))
+    acts_one, raw_one, shift_one, rate_one, start_grad = in_back(grad_heads)
+    all_grads = lax.all_gather(start_grad, "so", axis=0)
+    end_grad = jnp.zeros_like(start_grad)
+    for i in range(n - 1, 0, -1):
+        step = all_grads[i] + all_factors[i][:, :, None, None] * end_grad
+        end_grad = jnp.where(i > b, step, end_grad)
+    factor_grad = jnp.sum(end_grad * start_state, axis=(2, 3))
+    acts_two, raw_two, shift_two, rate_two = zero_back((grad_heads, factor_grad, end_grad))
+    skip_part = (grad_heads * skip[:, None]).reshape(2, length, XCOLS)
+    grad_acts = acts_one + acts_two + jnp.concatenate([skip_part, jnp.zeros((2, length, 2 * STATE), jnp.float32)], axis=2)
+    grad_ext, kern_grad, bias_grad = conv_back(grad_acts)
+    grad_dt = jnp.pad(raw_one + raw_two, ((0, 0), (margin, 0), (0, 128 - hl)))
+    gpc = jnp.concatenate([grad_ext, grad_dt], axis=2).astype(jnp.bfloat16)
+    gpg = grad_gate_z.astype(jnp.bfloat16)
+    wc_grad = jnp.einsum("qtd,qtk->dk", normed_low, gpc, preferred_element_type=jnp.float32)
+    wg_grad = jnp.einsum("qtd,qtk->dk", normed_low[:, margin:], gpg, preferred_element_type=jnp.float32)
+    grad_normed = jnp.einsum("qtk,dk->qtd", gpc, wc, preferred_element_type=jnp.float32)
+    late = grad_normed[:, margin:] + jnp.einsum("qtk,dk->qtd", gpg, wg, preferred_element_type=jnp.float32)
+    early = lax.ppermute(grad_normed[:, :margin], "so", down)
+    grad_normed = late + jnp.pad(early, ((0, 0), (length - margin, 0), (0, 0)))
+    grad_normed = lax.psum_scatter(grad_normed.reshape(4, own, -1), group, scatter_dimension=0, tiled=False)
+    _, pre_back = jax.vjp(rms_scale, tok.astype(jnp.float32), gain1)
+    grad_tokens_norm, pre_gain_grad = pre_back(grad_normed)
+    tokens_grad = cot.astype(jnp.float32) + grad_tokens_norm
+
+    low = lambda v: v.astype(jnp.bfloat16)
+    lead = (size["dpo"], 2, size["so"] * 2 * rows)
+    oc, og, oo = reduce(
+        size, low(wc_grad).reshape(lead + (CCOLS,)), low(wg_grad).reshape(lead + (XCOLS,)),
+        low(out_weight_grad).reshape(size["dpo"], size["so"] // 2, 2 * out_weight.shape[0], -1),
+    )
+    oc, og = oc.astype(jnp.float32), og.astype(jnp.float32)
+    by_class = lambda v: join_classes(v.reshape((2, 2) + v.shape[1:]), size)
+    in_weight_grad = jnp.concatenate([
+        by_class(og), by_class(oc[:, :, :XCOLS]), jnp.sum(oc[:, :, XCOLS : XCOLS + 2 * STATE], axis=0),
+        by_class(oc[:, :, XCOLS + 2 * STATE : XCOLS + 2 * STATE + hl]),
+    ], axis=1)
+    def place_class(v):
+        parts = jnp.zeros((2, 2) + v.shape, jnp.float32)
+        return join_classes(lax.dynamic_update_slice(parts, v[None, None], (c, s) + (0,) * v.ndim), size)
+    kern_grad = jnp.concatenate([place_class(kern_grad[:, :XCOLS]), kern_grad[:, XCOLS:]], axis=1).T
+    bias_grad = jnp.concatenate([place_class(bias_grad[:XCOLS]), bias_grad[XCOLS:]])
+    scattered = lambda v: lax.psum_scatter(v, AXES, scatter_dimension=0, tiled=True)
+    heads = lax.psum((place_class(shift_one + shift_two), place_class(rate_one + rate_two), place_class(skip_grad)), AXES)
+    return (
+        mixed[None], tokens_grad[None], scattered(pre_gain_grad), in_weight_grad, scattered(kern_grad), scattered(bias_grad),
+        heads[0], heads[1], heads[2], scattered(place_class(norm_gain_grad)), oo.astype(jnp.float32),
+    )
+
+
+def specs(dp, seq):
+    both = dp + seq
+    ins = (
+        P(dp, seq, None), P(dp, seq), P(both), P(both, None), P(both, None), P(both),
+        P(), P(), P(), P(both), P(both, None), P(dp, seq, None),
+    )
+    outs = (
+        P(dp, seq, None), P(dp, seq, None), P(both), P(both, None), P(both, None), P(both),
+        P(), P(), P(), P(both), P(both, None),
+    )
+    return ins, outs
+
 
 def solution(mesh):
-    return jax.shard_map(
-        body,
-        mesh=mesh,
-        in_specs=(
-            P("dp", "seq", None),
-            P("dp", "seq"),
-            P(("dp", "seq")),
-            P(("dp", "seq"), None),
-            P(("dp", "seq"), None),
-            P(("dp", "seq")),
-            P(),
-            P(),
-            P(),
-            P(("dp", "seq")),
-            P(("dp", "seq"), None),
-            P("dp", "seq", None),
-        ),
-        out_specs=(
-            P("dp", "seq", None),
-            P("dp", "seq", None),
-            P(("dp", "seq")),
-            P(("dp", "seq"), None),
-            P(("dp", "seq"), None),
-            P(("dp", "seq")),
-            P(),
-            P(),
-            P(),
-            P(("dp", "seq")),
-            P(("dp", "seq"), None),
-        ),
-        check_vma=False,
-    )
+    dp, seq = mesh.shape["dp"], mesh.shape["seq"]
+    fine = Mesh(mesh.devices.reshape(dp // 2, 2, seq // 2, 2), AXES)
+    size = dict(fine.shape)
+
+    def choose(*args):
+        in_rows, out_rows, own = args[3].shape[0], args[10].shape[0], args[0].shape[1]
+        ok = (args[0].shape[0] == 2 * size["dpo"] and own == 2 * size["so"] * GROUP and INNER % (dp * seq * HEADDIM // 2) == 0 and (in_rows // (dp * seq)) % 16 == 0 and size["so"] % 2 == 0)
+        if ok:
+            ins, outs = specs(AXES[:2], AXES[2:])
+            return jax.shard_map(functools.partial(fast_body, size), mesh=fine, in_specs=ins, out_specs=outs, check_vma=False)(*args)
+        ins, outs = specs(("dp",), ("seq",))
+        return jax.shard_map(whole_body, mesh=mesh, in_specs=ins, out_specs=outs, check_vma=False)(*args)
+
+    return choose

time: 1510 us -> 1000 us (0.66)
  waiting for transfers between devices: 931 us -> 133 us
  Pallas kernels: 0 us -> 290 us
  local copies, waits for them, and re-layouts: 55.2 us -> 122 us
  blocking collectives: 185 us -> 125 us
  starting transfers between devices: 56.4 us -> 7.88 us
  other arithmetic: 99.4 us -> 125 us
    ppermute x17 -> x3, waiting for transfers between devices: 438 us -> 3.54 us  [the longest x1 3.53 us: fast_body(): early = lax.ppermute(grad_normed[:, :margin], 'so', down)]
    reduce_scatter x3 -> x2, waiting for transfers between devices: 300 us -> 0.02 us  [the longest x1 0.02 us: fast_body(): lax.psum_scatter(branch.reshape(4, own, -1), group, scatter_dimension=0,...]
    pallas_call x0 -> x2, Pallas kernels: none -> 290 us  [the longest x1 159 us: gather(): pl.pallas_call(functools.partial(gather_kernel, size), out_shape=shapes,...]
    unnamed x9 -> x6, waiting for transfers between devices: 179 us -> 120 us
    ppermute x17 -> x3, starting transfers between devices: 56.1 us -> 7.05 us  [the longest x1 2.94 us: fast_body(): halo = lax.ppermute(toks[:, 2 * own - margin:], 'so', up)]
    unnamed x3 -> x1, blocking collectives: 83.1 us -> 43.8 us
    psum x1, blocking collectives: 40.6 us -> 8.25 us  [fast_body(): lax.psum(jnp.stack([jnp.sum(v * v, axis=-1), jnp.sum(u * v, axis=-1)]), g...]
    another operation x11 -> x19, other arithmetic: 9.74 us -> 35.3 us  [the longest x18 34.7 us: choose(): jax.shard_map(functools.partial(fast_body, size), mesh=fine, in_specs=ins...]
  transfers between devices with their start and end apart: 24 -> 8, of which waited for: 19 -> 3; matrix products, arithmetic and copies ran while one was open for 20% -> 20% of each run, Pallas kernels for 0% -> 13%
where the time goes in v1:
time: 1000 us; the launch traced here: 992 us
  Pallas kernels  290 us (29%)
  matrix products  172 us (17%)
  waiting for transfers between devices  133 us (13%)
  blocking collectives  125 us (12%)
  other arithmetic  125 us (12%)
  local copies, waits for them, and re-layouts  122 us (12%)
  between operations  16.4 us (2%)
    pallas_call x1, Pallas kernels, gather(): pl.pallas_call(functools.partial(gather_kernel, size), out_shape=shapes,...  159 us
    pallas_call x1, Pallas kernels, reduce(): pl.pallas_call(functools.partial(reduce_kernel, size), out_shape=outs, in...  131 us
    unnamed x6, waiting for transfers between devices  120 us
    all_gather x1, blocking collectives, fast_body(): everywhere = lambda v: lax.all_gather(v, AXES, axis=0, tiled=True)  56.7 us
    dot_general x6, matrix products, group_math(): inside = jnp.einsum('tsh,shp->thp', mixing, heads_x, precision=HIGHEST)  52.6 us
    unnamed x1, blocking collectives  43.8 us
    another operation x18, other arithmetic, choose(): jax.shard_map(functools.partial(fast_body, size), mesh=fine, in_specs=ins...  34.7 us
  transfers between devices with their start and end apart: 8, of which 3 were waited for; matrix products, arithmetic and copies ran while one was open for 20% of the time, Pallas kernels for 13%

profile of v1, /device:TPU:1, one launch (start us, length us, event | category | flops | bytes accessed | tf_op | source)
XLA Modules:
  0.0 991.9 jit_solution(6104460556802550820)
XLA Ops:
  12.5 159.4 %shard_map.203 = (bf16[2,2,384,1152]{3,2,1,0:T(8,128)(2,1)}, bf16[2,2,384,768]{3,2,1,0:T(8,128)(2,1)}, bf16[2,2,192,1536]{3,2,1,0:T(8,128)(2,1)}, bf16[4,256,1536]{2,1,0:T(8,128)(2,1)}, bf16[4,256,1536]{2,1,0:T(8,128)(2,1)}) custom-call(bf16[4,48,1152]{2,1,0:T(8,128)(2,1)} %concatenate.33.wc_in, bf16[4,48,768]{2,1,0:T(8,128)(2,1)} %reshape_reshape.28.wg_in, ...), custom_call_target="tpu_custom_call" | custom-call | tf_op jit(solution)/shard_map/pallas_call | solution.py:436
  176.4 7.9 all-gather.2
  187.3 56.7 %all-gather.3 = bf16[32,104,4]{1,2,0:T(4,128)(2,1)S(1)} all-gather(bf16[1,104,4]{1,2,0:T(4,128)(2,1)S(1)} %bitcast.630), channel_id=1, replica_groups=mesh['dpo'=2,'dpi'=2,'so'=4,'si'=2] {'dpo','dpi','so','si'}, dimensions={0}, use_global_device_ids=true | all-gather | bytes 27456 | tf_op jit(solution)/shard_map/all_gather | solution.py:595
  244.9 43.8 %all-reduce.37 = (bf16[1536]{0:T(1024)(128)(2,1)S(1)}, bf16[3328]{0:T(1024)(128)(2,1)S(1)}, bf16[3072]{0:T(1024)(128)(2,1)S(1)}) all-reduce(bf16[1536]{0:T(1024)(128)(2,1)S(1)} %dynamic-update-slice.1, bf16[3328]{0:T(1024)(128)(2,1)S(1)} %dynamic-update-slice, ...), channel_id=1, replica_groups=mesh['dpo'=2,'dpi'=2,'so'=4,'si'=2] {'dpo','dpi','so','si'}, use_global_device_ids=true, to_apply=%add.30 | all-reduce | flops 7936 | bytes 31744
  299.2 7.0 fusion.247
  306.3 5.2 fusion.24
  329.7 3.5 reshape.806
  333.3 7.8 fusion.260
  354.1 3.4 fusion.115
  377.4 7.5 fusion.86
  385.0 7.5 fusion.87
  395.8 8.8 all_gather.35
  409.1 4.3 fusion.66
  413.4 9.9 all-gather.7.cloned.1.call-done
  425.9 5.8 multiply_add_fusion.1
  434.1 9.1 multiply_reduce_fusion.10
  443.8 8.2 psum.28
  452.1 8.3 multiply_reduce_fusion.7
  462.8 4.8 fusion.61
  471.1 3.7 reshape_reshape.30
  479.3 11.2 %reduce-window.50 = f32[2,12,4,128]{3,1,2,0:T(8,128)} reduce-window(f32[2,12,4,128]{3,1,2,0:T(8,128)} %copy.542, f32[]{:T(128)} %constant.211.clone.1), window={size=1x1x1x128 pad=0_0x0_0x0_0x0_127}, to_apply=%region_15.17 | reduce-window | flops 1560576 | bytes 98308 | tf_op jit(solution)/shard_map/reduce-window.6 | solution.py:772
  498.8 11.3 %fusion.27 = (f32[2,256,12]{1,2,0:T(8,128)}, f32[2,256,12]{1,2,0:T(8,128)}, f32[2,256,12]{1,2,0:T(8,128)}, f32[2,256,256]{2,1,0:T(8,128)}) fusion(f32[2,256,12]{1,2,0:T(8,128)S(1)} %copy-done.96, f32[2,256,256]{2,1,0:T(8,128)S(1)} %copy-done.62, f32[2,256,256]{2,1,0:T(8,128)S(1)} %copy-done.58, f32[2,256,12]{1,2,0:T(8,128)S(1)} %copy-done.92, ...), kind=kOutput, calls=%fused_computation.55 | convolution fusion | flops 1231403008 | bytes 5021696 | tf_op jit(solution)/shard_map/transpose(jvp(vmap(tsh,shp->thp)))/dot_general | solution.py:51
  511.7 4.2 fusion.85
  519.8 13.0 %fusion.25 = (f32[2,256,12]{1,2,0:T(8,128)}, f32[2,256,12]{1,2,0:T(8,128)}, f32[2,256,12]{1,2,0:T(8,128)}, f32[2,256,256]{2,1,0:T(8,128)}) fusion(f32[2,256,12]{1,2,0:T(8,128)} %copy.515, f32[2,256,256]{2,1,0:T(8,128)} %copy-done.59, f32[2,256,256]{2,1,0:T(8,128)} %get-tuple-element.117, f32[2,256,12]{1,2,0:T(8,128)} %copy.511, ...), kind=kOutput, calls=%fused_computation.53 | convolution fusion | flops 1231403008 | bytes 5021696 | tf_op jit(solution)/shard_map/transpose(jvp(vmap(tsh,shp->thp)))/dot_general | solution.py:51
  539.0 4.2 fusion.140
  544.9 3.9 fusion.139
  550.3 5.9 fusion.122
  558.1 4.3 multiply_reduce_fusion.15
  571.3 3.4 fusion.133
  574.7 3.4 fusion.136
  582.1 3.7 fusion.256
  588.8 5.4 reduce-window.56
  599.2 5.0 reduce-window.54
  605.7 7.4 fusion.75
  613.1 5.9 fusion.79
  621.7 3.6 reshape.835
  632.7 9.8 multiply_reduce_fusion.5
  647.8 5.8 add_convert_fusion
  653.7 7.2 fusion.142
  662.2 3.5 collective-permute-done.2
  665.7 4.7 fusion.4
  670.7 7.5 fusion.265
  682.2 6.8 bitcast_convert_fusion
  689.0 4.0 bitcast_convert_fusion.1
  693.0 7.8 fusion
  700.8 130.9 %shard_map.204 = (bf16[4,48,1152]{2,1,0:T(8,128)(2,1)}, bf16[4,48,768]{2,1,0:T(8,128)(2,1)}, bf16[96,1536]{1,0:T(8,128)(2,1)}) custom-call(bf16[2,2,384,1152]{3,2,1,0:T(8,128)(2,1)} %bitcast.565, bf16[2,2,384,768]{3,2,1,0:T(8,128)(2,1)} %bitcast.570, bf16[2,2,192,1536]{3,2,1,0:T(8,128)(2,1)} %bitcast.569), custom_call_target="tpu_custom_call" | custom-call | tf_op jit(solution)/shard_map/pallas_call | solution.py:545
  853.6 3.4 fusion.74
  857.0 119.5 %all-reduce.40.cloned.1.call-done = (f32[1536]{0:T(1024)}, f32[3328,4]{0,1:T(4,128)}, f32[3328]{0:T(1024)}, f32[48]{0:T(128)}, f32[48]{0:T(128)}, /*index=5*/f32[48]{0:T(128)}, f32[3072]{0:T(1024)}) async-done(((f32[1536]{0:T(1024)}, f32[3328,4]{0,1:T(4,128)}, f32[3328]{0:T(1024)}, f32[48]{0:T(128)}, f32[48]{0:T(128)}, /*index=5*/f32[48]{0:T(128)}, f32[3072]{0:T(1024)}), (f32[1536]{0:T(1024)}, ...) | async-done | bytes 85584
  (593 shorter events, 196.0 us)
Async XLA Ops:
  7.2 416.1 %all-gather.7.cloned.1.call-start = ((), (), s32[]{:S(2)}) async-start(), calls=%async_computation.4 | async-start | bytes 3932160 | tf_op jit(solution)/shard_map/all_gather | solution.py:670
  9.4 167.0 %copy-start.136 = (s32[1,256]{1,0:T(1,128)S(1)}, s32[1,256]{1,0:T(1,128)}, u32[]{:S(2)}) copy-start(s32[1,256]{1,0:T(1,128)} %param.14) | copy-start | bytes 3076
  9.4 177.9 %copy-start.137 = (bf16[104,4]{0,1:T(4,128)(2,1)S(1)}, bf16[104,4]{0,1:T(4,128)(2,1)}, u32[]{:S(2)}) copy-start(bf16[104,4]{0,1:T(4,128)(2,1)} %param.17) | copy-start | bytes 2500
  9.7 234.4 %copy-start.143 = (bf16[48]{0:T(256)(128)(2,1)S(1)}, bf16[48]{0:T(256)(128)(2,1)}, u32[]{:S(2)}) copy-start(bf16[48]{0:T(256)(128)(2,1)} %param.15) | copy-start | bytes 292
  9.7 234.7 %copy-start.144 = (bf16[104]{0:T(256)(128)(2,1)S(1)}, bf16[104]{0:T(256)(128)(2,1)}, u32[]{:S(2)}) copy-start(bf16[104]{0:T(256)(128)(2,1)} %param.18) | copy-start | bytes 628
  9.7 234.9 %copy-start.145 = (bf16[96]{0:T(256)(128)(2,1)S(1)}, bf16[96]{0:T(256)(128)(2,1)}, u32[]{:S(2)}) copy-start(bf16[96]{0:T(256)(128)(2,1)} %param.22) | copy-start | bytes 580
  9.8 279.3 %copy-start.138 = (f32[48]{0:T(128)S(1)}, f32[48]{0:T(128)}, u32[]{:S(2)}) copy-start(f32[48]{0:T(128)} %param.19) | copy-start | bytes 580
  9.8 279.5 %copy-start.139 = (f32[48]{0:T(128)S(1)}, f32[48]{0:T(128)}, u32[]{:S(2)}) copy-start(f32[48]{0:T(128)} %param.20) | copy-start | bytes 580
  10.3 280.1 %copy-start.140 = (f32[48]{0:T(128)S(1)}, f32[48]{0:T(128)}, u32[]{:S(2)}) copy-start(f32[48]{0:T(128)} %param.21) | copy-start | bytes 580
  171.9 125.4 %copy-start.17 = (bf16[4,256,1536]{2,1,0:T(8,128)(2,1)S(1)}, bf16[4,256,1536]{2,1,0:T(8,128)(2,1)}, u32[]{:S(2)}) copy-start(bf16[4,256,1536]{2,1,0:T(8,128)(2,1)} %get-tuple-element.21) | copy-start | bytes 9437188
  173.5 123.8 %collective-permute-start.1 = (bf16[2,3,1536]{2,1,0:T(4,128)(2,1)}, bf16[2,3,1536]{2,1,0:T(4,128)(2,1)}, u32[]{:S(2)}, u32[]{:S(2)}) collective-permute-start(bf16[2,3,1536]{2,1,0:T(4,128)(2,1)} %slice.347), channel_id=1, source_target_pairs={{0,2},{2,4},{4,6},{1,3},{3,5},{5,7},{8,10},{10,12},{12,14},{9,11},... | collective-permute-start | bytes 55304 | tf_op jit(solution)/shard_map/ppermute | solution.py:612
  184.5 109.0 %collective-permute-start = (s32[2,3]{1,0:T(2,128)S(1)}, s32[2,3]{1,0:T(2,128)S(1)}, u32[]{:S(2)}, u32[]{:S(2)}) collective-permute-start(s32[2,3]{1,0:T(2,128)S(1)} %slice.344), channel_id=1, source_target_pairs={{0,2},{2,4},{4,6},{1,3},{3,5},{5,7},{8,10},{10,12},{12,14},{9,11},... | collective-permute-start | bytes 80 | tf_op jit(solution)/shard_map/ppermute | solution.py:613
  293.3 22.3 %copy-start.126 = (f32[12]{0:T(128)}, f32[12]{0:T(128)S(1)}, u32[]{:S(2)}) copy-start(f32[12]{0:T(128)S(1)} %get-tuple-element.155) | copy-start | bytes 148
  293.3 22.3 %copy-start.128 = (f32[12]{0:T(128)}, f32[12]{0:T(128)S(1)}, u32[]{:S(2)}) copy-start(f32[12]{0:T(128)S(1)} %get-tuple-element.154) | copy-start | bytes 148
  293.4 12.9 %copy-start.81 = (f32[1,1024]{1,0:T(1,128)}, f32[1,1024]{1,0:T(1,128)S(1)}, u32[]{:S(2)}) copy-start(f32[1,1024]{1,0:T(1,128)S(1)} %get-tuple-element.119) | copy-start | bytes 12292
  293.4 12.9 %copy-start.83 = (f32[1,1024]{1,0:T(1,128)}, f32[1,1024]{1,0:T(1,128)S(1)}, u32[]{:S(2)}) copy-start(f32[1,1024]{1,0:T(1,128)S(1)} %get-tuple-element.120) | copy-start | bytes 12292
  293.4 12.9 %copy-start.85 = (f32[1,1024]{1,0:T(1,128)}, f32[1,1024]{1,0:T(1,128)S(1)}, u32[]{:S(2)}) copy-start(f32[1,1024]{1,0:T(1,128)S(1)} %get-tuple-element.121) | copy-start | bytes 12292
  293.4 12.9 %copy-start.87 = (f32[1,1024]{1,0:T(1,128)}, f32[1,1024]{1,0:T(1,128)S(1)}, u32[]{:S(2)}) copy-start(f32[1,1024]{1,0:T(1,128)S(1)} %get-tuple-element.122) | copy-start | bytes 12292
  293.5 140.6 %copy-start.112 = (f32[768]{0:T(1024)}, f32[768]{0:T(1024)S(1)}, u32[]{:S(2)}) copy-start(f32[768]{0:T(1024)S(1)} %get-tuple-element.152) | copy-start | bytes 9220
  293.8 12.5 %copy-start.97 = (pred[2,512]{1,0:T(4,128)(4,1)}, pred[2,512]{1,0:T(4,128)(4,1)S(1)}, u32[]{:S(2)}) copy-start(pred[2,512]{1,0:T(4,128)(4,1)S(1)} %get-tuple-element.125) | copy-start | bytes 3076
  293.8 12.5 %copy-start.99 = (pred[2,512]{1,0:T(4,128)(4,1)}, pred[2,512]{1,0:T(4,128)(4,1)S(1)}, u32[]{:S(2)}) copy-start(pred[2,512]{1,0:T(4,128)(4,1)S(1)} %get-tuple-element.126) | copy-start | bytes 3076
  293.9 12.5 %copy-start.101 = (pred[2,512]{1,0:T(4,128)(4,1)}, pred[2,512]{1,0:T(4,128)(4,1)S(1)}, u32[]{:S(2)}) copy-start(pred[2,512]{1,0:T(4,128)(4,1)S(1)} %get-tuple-element.127) | copy-start | bytes 3076
  293.9 101.2 %copy-start.79 = (f32[2,512]{1,0:T(2,128)}, f32[2,512]{1,0:T(2,128)S(1)}, u32[]{:S(2)}) copy-start(f32[2,512]{1,0:T(2,128)S(1)} %get-tuple-element.132) | copy-start | bytes 12292
  357.5 200.6 %all-gather.9.cloned.1.call-start = ((), (), s32[]{:S(2)}) async-start(), calls=%async_computation.5 | async-start | bytes 3932160 | tf_op jit(solution)/shard_map/all_gather | solution.py:700
  371.4 13.5 %copy-start.59 = (f32[2,256,256]{2,1,0:T(8,128)}, f32[2,256,256]{2,1,0:T(8,128)S(1)}, u32[]{:S(2)}) copy-start(f32[2,256,256]{2,1,0:T(8,128)S(1)} %fusion.174) | copy-start | bytes 1572868
  373.2 11.7 %copy-start.61 = (f32[2,256,256]{2,1,0:T(8,128)}, f32[2,256,256]{2,1,0:T(8,128)S(1)}, u32[]{:S(2)}) copy-start(f32[2,256,256]{2,1,0:T(8,128)S(1)} %fusion.181) | copy-start | bytes 1572868
  393.0 12.2 %copy-start.18 = (bf16[4,256,1536]{2,1,0:T(8,128)(2,1)S(1)}, bf16[4,256,1536]{2,1,0:T(8,128)(2,1)}, u32[]{:S(2)}) copy-start(bf16[4,256,1536]{2,1,0:T(8,128)(2,1)} %get-tuple-element.21) | copy-start | bytes 9437188
  393.0 12.2 %copy-start.104 = (f32[2,515]{1,0:T(2,128)S(1)}, f32[2,515]{1,0:T(2,128)}, u32[]{:S(2)}) copy-start(f32[2,515]{1,0:T(2,128)} %copy-done.103) | copy-start | bytes 12364
  409.1 14.2 %copy-start.123 = (f32[2,12]{1,0:T(2,128)S(1)}, f32[2,12]{1,0:T(2,128)}, u32[]{:S(2)}) copy-start(f32[2,12]{1,0:T(2,128)} %get-tuple-element.129) | copy-start | bytes 292
  467.7 382.6 %reduce-scatter.6.cloned.1.call-start = ((), (), s32[]{:S(2)}) async-start(), calls=%async_computation.3 | async-start | bytes 7864320 | tf_op jit(solution)/shard_map/reduce_scatter | solution.py:719
  498.7 11.4 %copy-start.1 = (f32[2,2,256,12,64]{2,4,3,0,1:T(8,128)}, f32[2,2,256,12,64]{2,4,3,0,1:T(8,128)S(1)}, u32[]{:S(2)}) copy-start(f32[2,2,256,12,64]{2,4,3,0,1:T(8,128)S(1)} %copy.684) | copy-start | bytes 9437188
  519.8 16.2 %copy-start.107 = (f32[2,256]{1,0:T(2,128)S(1)}, f32[2,256]{1,0:T(2,128)}, u32[]{:S(2)}) copy-start(f32[2,256]{1,0:T(2,128)} %copy-done.106) | copy-start | bytes 6148
  571.3 10.8 %copy-start.117 = (f32[2,12]{1,0:T(2,128)S(1)}, f32[2,12]{1,0:T(2,128)}, u32[]{:S(2)}) copy-start(f32[2,12]{1,0:T(2,128)} %slice_bitcast_fusion.6) | copy-start | bytes 292
  571.3 10.8 %copy-start.119 = (f32[2,12]{1,0:T(2,128)S(1)}, f32[2,12]{1,0:T(2,128)}, u32[]{:S(2)}) copy-start(f32[2,12]{1,0:T(2,128)} %slice_bitcast_fusion.7) | copy-start | bytes 292
  585.8 19.7 %copy-start.121 = (f32[2,12]{1,0:T(2,128)S(1)}, f32[2,12]{1,0:T(2,128)}, u32[]{:S(2)}) copy-start(f32[2,12]{1,0:T(2,128)} %get-tuple-element.79) | copy-start | bytes 292
  585.8 19.7 %copy-start.134 = (f32[2]{0:T(128)S(1)}, f32[2]{0:T(128)}, u32[]{:S(2)}) copy-start(f32[2]{0:T(128)} %get-tuple-element.55) | copy-start | bytes 28
  585.8 19.7 %copy-start.135 = (f32[2,12]{1,0:T(2,128)S(1)}, f32[2,12]{1,0:T(2,128)}, u32[]{:S(2)}) copy-start(f32[2,12]{1,0:T(2,128)} %get-tuple-element.50) | copy-start | bytes 292
  585.8 19.8 %copy-start.68 = (f32[2,256,12]{1,2,0:T(8,128)S(1)}, f32[2,256,12]{1,2,0:T(8,128)}, u32[]{:S(2)}) copy-start(f32[2,256,12]{1,2,0:T(8,128)} %copy.517) | copy-start | bytes 73732
  632.6 9.9 copy-start.82
  632.6 9.9 copy-start.84
  632.7 9.9 copy-start.86
  632.7 9.9 copy-start.88
  642.5 193.1 %copy-start.77 = (f32[1024]{0:T(1024)}, f32[1024]{0:T(1024)S(1)}, u32[]{:S(2)}) copy-start(f32[1024]{0:T(1024)S(1)} %get-tuple-element.34) | copy-start | bytes 12292
  653.7 12.0 %copy-start.43 = (bf16[2,512,768]{2,1,0:T(8,128)(2,1)S(1)}, bf16[2,512,768]{2,1,0:T(8,128)(2,1)}, u32[]{:S(2)}) copy-start(bf16[2,512,768]{2,1,0:T(8,128)(2,1)} %get-tuple-element.84) | copy-start | bytes 4718596
  653.7 12.0 %copy-start.142 = (bf16[2,2,384,768]{3,2,1,0:T(8,128)(2,1)S(1)}, bf16[2,2,384,768]{3,2,1,0:T(8,128)(2,1)}, u32[]{:S(2)}) copy-start(bf16[2,2,384,768]{3,2,1,0:T(8,128)(2,1)} %get-tuple-element.24) | copy-start | bytes 7077892
  660.9 4.8 collective-permute-start.2
  670.4 183.1 %reduce-scatter.4.cloned.1.call-start = ((), (), s32[]{:S(2)}) async-start(), calls=%async_computation.2 | async-start | bytes 7864320 | tf_op jit(solution)/shard_map/reduce_scatter | solution.py:694
  678.2 298.3 %all-reduce.40.cloned.1.call-start = ((), (), s32[]{:S(2)}) async-start(), calls=%async_computation.6 | async-start | bytes 183296
  (108 other events, 553.5 us)
Sparse Core Ops, SparseCore 0:
  357.6 65.6 all-gather.6
  467.8 61.2 all-gather.8
  670.6 57.3 reduce-scatter.5
  730.5 58.3 reduce-scatter.3
  853.7 122.7 all-reduce.39

commit v2 on v0

--- a/solution.py
+++ b/solution.py
@@ -1,6 +1,12 @@
+import functools
+import types
+
 import jax
 import jax.numpy as jnp
 from jax import lax
+from jax.experimental import pallas as pl
+from jax.experimental.pallas import tpu as pltpu
+from jax.sharding import Mesh
 from jax.sharding import PartitionSpec as P
 
 HEADS = 48
@@ -67,7 +73,7 @@
     )
 
 
-def body(
+def whole_body(
     tokens,
     segment_ids,
     pre_gain,
@@ -254,37 +260,1447 @@
         sums[5],
     )
 
+AXES = ("dpo", "dpi", "so", "si")
+MESH = pl.DeviceIdType.MESH
+XCOLS = INNER // 4
+ACT = XCOLS + 2 * STATE
+CCOLS = ACT + 128
+CHUNK = 128
+HL = HEADS // 4
+PAD = 16
+MARGIN = CONVW - 1
+f32, bf16 = jnp.float32, jnp.bfloat16
+VMEM = pl.BlockSpec(memory_space=pltpu.VMEM)
+HBM = pl.BlockSpec(memory_space=pl.ANY)
+
+
+def guarded(when, action):
+    if when is None:
+        action()
+    else:
+        pl.when(when)(action)
+
+
+class Wires:
+    def __init__(self, send, recv, local):
+        self.send, self.recv, self.local = send, recv, local
+        self.used, self.kept, self.pending = 0, 0, []
+
+    def slot(self):
+        self.used += 1
+        return self.used - 1
+
+    def copy(self, src, dst, slot, device, landed=None):
+        return pltpu.make_async_remote_copy(
+            src_ref=src, dst_ref=dst, send_sem=self.send.at[slot],
+            recv_sem=self.recv.at[slot if landed is None else landed],
+            device_id=device, device_id_type=MESH,
+        )
+
+    def start(self, src, dst, slot, device, when=None, landed=None):
+        copy = self.copy(src, dst, slot, device, landed)
+        guarded(when, copy.start)
+        self.pending.append((copy, when))
+        return self.pending[-1]
+
+    def sent(self, entry):
+        self.pending = [kept for kept in self.pending if kept is not entry]
+        guarded(entry[1], entry[0].wait_send)
+
+    def arrived(self, landing, slot, device, when=None):
+        guarded(when, self.copy(landing, landing, slot, device).wait_recv)
+
+    def keep(self, src, dst, when=None):
+        copy = pltpu.make_async_copy(src, dst, self.local.at[self.kept])
+        self.kept += 1
+        guarded(when, copy.start)
+        return lambda: guarded(when, copy.wait)
+
+    def finish(self):
+        for copy, when in self.pending:
+            guarded(when, copy.wait_send)
+        self.pending = []
+
+
+def place():
+    return tuple(lax.axis_index(name) for name in AXES)
+
+
+def member(here, rel):
+    a, c, b, s = here
+    return (a, c ^ (rel >> 1), b, s ^ (rel & 1))
+
+
+def greet(here, size, extra):
+    a, c, b, s = here
+    n, nx = size["so"], size["dpo"]
+    barrier = pltpu.get_barrier_semaphore()
+    known = [member(here, rel) for rel in range(1, 4)]
+    known += [(a, c, lax.rem(b + k, n), s) for k in range(1, n)]
+    known += [(lax.rem(a + k, nx), c, b, s) for k in range(1, nx)]
+    for device in known:
+        pl.semaphore_signal(barrier, inc=1, device_id=device, device_id_type=MESH)
+    met = len(known)
+    for devices, when in extra:
+        for device in devices:
+            guarded(when, lambda device=device: pl.semaphore_signal(barrier, inc=1, device_id=device, device_id_type=MESH))
+        met = met + len(devices) * when.astype(jnp.int32)
+    return lambda: pl.semaphore_wait(barrier, met)
+
+
+def mm(x, y, dims=((1,), (0,)), exact=None):
+    if exact is not None:
+        whole = (x, y)[exact].astype(f32)
+        high = whole.astype(bf16)
+        low = (whole - high.astype(f32)).astype(bf16)
+        parts = [(high, y), (low, y)] if exact == 0 else [(x, high), (x, low)]
+        return mm(*parts[0], dims) + mm(*parts[1], dims)
+    return lax.dot_general(x.astype(bf16), y.astype(bf16), (dims, ((), ())), preferred_element_type=f32)
+
+
+def fine(x, y, dims=((1,), (0,))):
+    x, y = x.astype(f32), y.astype(f32)
+    xh, yh = x.astype(bf16), y.astype(bf16)
+    xl, yl = (x - xh.astype(f32)).astype(bf16), (y - yh.astype(f32)).astype(bf16)
+    return mm(xh, yh, dims) + (mm(xl, yh, dims) + mm(xh, yl, dims))
+
+
+def iota(shape, axis):
+    return lax.broadcasted_iota(jnp.int32, shape, axis)
+
+
+def spread_heads():
+    return (iota((128, XCOLS), 0) == iota((128, XCOLS), 1) // HEADDIM).astype(f32).astype(bf16)
+
+
+def gather_heads():
+    return (iota((XCOLS, 128), 1) == iota((XCOLS, 128), 0) // HEADDIM).astype(f32).astype(bf16)
+
+
+def class_heads(size, cc, ss):
+    per = size["so"] // 2
+    run = HEADS // (size["dpo"] * 4 * per)
+    lane = iota((128, 128), 1)
+    group, j = lane // run, lane % run
+    head = (((group // per * 2 + cc) * per + group % per) * 2 + ss) * run + j
+    return ((iota((128, 128), 0) == head) & (lane < HL)).astype(f32).astype(bf16)
+
+
+def pick_heads(values, chosen, dims=((1,), (0,))):
+    high = values.astype(bf16)
+    rest = values - high.astype(f32)
+    middle = rest.astype(bf16)
+    low = rest - middle.astype(f32)
+    return mm(high, chosen, dims) + mm(middle, chosen, dims) + mm(low, chosen, dims)
+
+
+def loop(count, body, first=0):
+    lax.fori_loop(first, count, lambda i, _: (body(i), 0)[1], 0)
+
+
+def chunk_rows(r, i):
+    per = r.span // CHUNK
+    flat = pl.multiple_of(i * CHUNK, CHUNK)
+    padded = pl.multiple_of((i // per) * (r.span + PAD) + PAD + (i % per) * CHUNK, PAD)
+    return flat, padded
+
+
+def chunk_decays(r, i):
+    flat, padded = chunk_rows(r, i)
+    rows = pl.ds(flat, CHUNK)
+    ids = r.idc[pl.ds(padded, CHUNK), :]
+    before = r.idc[pl.ds(pl.multiple_of(padded - 8, 8), 8), :][7:8]
+    last = ids[CHUNK - 1 : CHUNK]
+    return flat, padded, rows, ids, before, last
+
+
+def phase_norm(r, i, block):
+    rows = pl.ds(pl.multiple_of(i * block, 16), block)
+    t = r.toks[rows, :].astype(f32)
+    scale = lax.rsqrt(jnp.mean(t * t, axis=1, keepdims=True) + EPSILON)
+    r.normed[rows, :] = (t * scale * r.gain1[0:1]).astype(bf16)
+
+
+def taps(window, ids, k, rows):
+    first = 8 - MARGIN + k
+    same = ids[first : first + rows] == ids[8 : 8 + rows]
+    return jnp.where(same, window[first : first + rows], 0.0)
+
+
+def phase_in(r, q, w, first):
+    rows = r.span + PAD
+    w = w.reshape(w.shape[0] * w.shape[1], 256)
+    r.pc[q * rows : (q + 1) * rows, pl.ds(first, 256)] = mm(r.normed[q * rows : (q + 1) * rows, :], w)
+    ids = r.idc[q * rows + PAD - 8 : (q + 1) * rows, :]
+    for half in range(2):
+        tile = pl.ds(pl.multiple_of(first + half * 128, 128), 128)
+        window = r.pc[q * rows + PAD - 8 : (q + 1) * rows, tile]
+        kern = r.cv[:, tile]
+        pre = kern[4:5] + window[8:] * kern[3:4]
+        for k in range(MARGIN):
+            pre = pre + taps(window, ids, k, r.span) * kern[k : k + 1]
+        gate = jax.nn.sigmoid(pre)
+        act = pre * gate
+        r.act[q * r.span : (q + 1) * r.span, tile] = act
+        r.sp[q * r.span : (q + 1) * r.span, tile] = gate + act * (1.0 - gate)
+
+
+def phase_decay(r, i):
+    flat, padded, rows, ids, before, last = chunk_decays(r, i)
+    raw = r.dtr[pl.ds(padded, CHUNK), :] + r.hp[0:1]
+    lane = iota((CHUNK, 128), 1) < HL
+    dt = jnp.where(lane, jnp.maximum(raw, 0.0) + jnp.log1p(jnp.exp(-jnp.abs(raw))), 0.0)
+    la = -jnp.exp(r.hp[1:2]) * dt
+    tril = (iota((CHUNK, CHUNK), 0) >= iota((CHUNK, CHUNK), 1)).astype(f32)
+    run = mm(tril, la, exact=1)
+    end = run[CHUNK - 1 : CHUNK]
+    weight = jnp.where(ids == last, jnp.exp(end - run), 0.0)
+    passed = jnp.where(last == before, jnp.exp(end), 0.0)
+    e = spread_heads()
+    xdt = r.act[rows, 0:XCOLS] * mm(dt, e, exact=0)
+    xw = xdt * mm(weight, e, exact=0)
+    r.dtm[rows, :] = dt
+    r.run[rows, :] = run
+    r.xdt[rows, :] = xdt.astype(bf16)
+    r.st[i] = fine(r.act[rows, XCOLS : XCOLS + STATE], xw, ((0,), (0,)))
+    r.pex[i] = mm(jnp.broadcast_to(passed, (8, 128)), e, exact=0)
+
+
+def phase_states(r):
+    per = r.span // CHUNK
+    for q in range(2):
+        cur = jnp.zeros((STATE, XCOLS), f32)
+        fac = jnp.ones((8, XCOLS), f32)
+        for j in range(per):
+            i = q * per + j
+            fresh = r.st[i]
+            r.st[i] = cur
+            r.cum[i] = fac
+            cur = r.pex[i][0:1] * cur + fresh
+            fac = fac * r.pex[i]
+        r.end[q] = cur
+        r.fac[q] = fac
+
+
+def chunk_matrix(r, i):
+    flat, padded, rows, ids, before, last = chunk_decays(r, i)
+    mask = (ids == ids.T) & (iota((CHUNK, CHUNK), 0) >= iota((CHUNK, CHUNK), 1))
+    bm = r.bc[rows, 0:STATE].astype(bf16)
+    cm = r.bc[rows, STATE:].astype(bf16)
+    cb = mm(cm, bm, ((1,), (1,)))
+    run = r.run[rows, :]
+    return rows, mask, bm, cm, cb, run, run.T
+
+
+def phase_inside(r, i):
+    rows, mask, bm, cm, cb, run, runt = chunk_matrix(r, i)
+    for hp in range(HL // 2):
+        tile = pl.ds(hp * 128, 128)
+        xdt = r.xdt[rows, tile]
+        outs = []
+        for k in range(2):
+            h = 2 * hp + k
+            decay = jnp.exp(jnp.where(mask, run[:, h : h + 1] - runt[h : h + 1, :], -1e30))
+            outs.append(mm(decay * cb, xdt[:, k * HEADDIM : (k + 1) * HEADDIM]))
+        r.y[rows, tile] = jnp.concatenate(outs, axis=1)
+
+
+def phase_carried(r, i):
+    flat, padded, rows, ids, before, last = chunk_decays(r, i)
+    enter = mm(jnp.where(ids == before, jnp.exp(r.run[rows, :]), 0.0), spread_heads(), exact=0)
+    start = r.st[i] + r.cum[i][0:1] * r.sin[i // (r.span // CHUNK)]
+    r.st[i] = start
+    carried = fine(r.act[rows, XCOLS + STATE : ACT], start) * enter
+    r.y[rows, :] += carried + r.hx[0:1] * r.act[rows, 0:XCOLS]
+
+
+def column_pair(first, second):
+    lanes = iota((first.shape[0], 128), 1)
+    return jnp.where(lanes == 0, first, jnp.where(lanes == 1, second, 0.0)).T[0:8]
+
+
+def phase_sums(r, i):
+    rows = pl.ds(pl.multiple_of(i * CHUNK, CHUNK), CHUNK)
+    z = r.z[rows, :]
+    v = r.y[rows, :] * (z * jax.nn.sigmoid(z))
+    u = r.gg[rows, :] * r.ng[0:1]
+    r.sums[0, i] = column_pair(jnp.sum(v * v, axis=1, keepdims=True), jnp.sum(u * v, axis=1, keepdims=True))
+
+
+def phase_gate(r, i):
+    rows = pl.ds(pl.multiple_of(i * CHUNK, CHUNK), CHUNK)
+    total = (r.sums[0, i] + r.sums[1, i]) + (r.sums[2, i] + r.sums[3, i])
+    cols = jnp.concatenate([total, jnp.zeros((CHUNK - 8, 128), f32)], axis=0).T
+    scale = lax.rsqrt(cols[:, 0:1] / INNER + EPSILON)
+    tilt = scale * scale * scale * (cols[:, 1:2] / INNER)
+    z, y, gg = r.z[rows, :], r.y[rows, :], r.gg[rows, :]
+    gate = jax.nn.sigmoid(z)
+    silu = z * gate
+    v = y * silu
+    vr = v * scale
+    gv = gg * r.ng[0:1] * scale - v * tilt
+    r.gated[rows, :] = (vr * r.ng[0:1]).astype(bf16)
+    r.gpg[rows, :] = (gv * y * (gate + silu * (1.0 - gate))).astype(bf16)
+    r.gg[rows, :] = gv * silu
+    r.nggrad[0:1] += jnp.sum(gg * vr, axis=0, keepdims=True)
+
+
+def phase_back_states(r, i, x):
+    flat, padded, rows, ids, before, last = chunk_decays(r, i)
+    enter = mm(jnp.where(ids == before, jnp.exp(r.run[rows, :]), 0.0), spread_heads(), exact=0)
+    dy = r.gg[rows, :]
+    own = r.y[rows, :] - r.hx[0:1] * x
+    low = dy.astype(bf16).astype(f32)
+    r.drun[rows, :] = mm(low * own, gather_heads(), exact=0)
+    r.y[rows, :] = fine(r.bc[rows, STATE:], dy * enter, ((0,), (0,)))
+    r.tally[2:3] += jnp.sum(mm(dy * x, gather_heads(), exact=0), axis=0, keepdims=True)
+
+
+def phase_back_chain(r):
+    per = r.span // CHUNK
+    for q in range(2):
+        cur = jnp.zeros((STATE, XCOLS), f32)
+        fac = jnp.ones((8, XCOLS), f32)
+        for j in reversed(range(per)):
+            i = q * per + j
+            rows = slice(i * CHUNK, (i + 1) * CHUNK)
+            fresh = r.y[rows, :]
+            r.y[rows, :] = cur
+            r.cum[i] = fac
+            cur = r.pex[i][0:1] * cur + fresh
+            fac = fac * r.pex[i]
+        r.end[q] = cur
+
+
+def phase_back_inside(r, i):
+    rows, mask, bm, cm, cb, run, runt = chunk_matrix(r, i)
+    dcb = jnp.zeros((CHUNK, CHUNK), f32)
+    for hp in range(HL // 2):
+        tile = pl.ds(hp * 128, 128)
+        xdt, dy = r.xdt[rows, tile], r.gg[rows, tile].astype(bf16)
+        outs = []
+        for k in range(2):
+            h = 2 * hp + k
+            part = slice(k * HEADDIM, (k + 1) * HEADDIM)
+            decay = jnp.exp(jnp.where(mask, run[:, h : h + 1] - runt[h : h + 1, :], -1e30))
+            dcb = dcb + mm(dy[:, part], xdt[:, part], ((1,), (1,))) * decay
+            outs.append(mm(decay * cb, dy[:, part], ((0,), (0,))))
+        r.gx[rows, tile] = jnp.concatenate(outs, axis=1)
+    r.gbc[rows, 0:STATE] = mm(dcb, cm, ((0,), (0,)))
+    r.gbc[rows, STATE : 2 * STATE] = mm(dcb, bm)
+
+
+def phase_back_close(r, i, start, x):
+    flat, padded, rows, ids, before, last = chunk_decays(r, i)
+    q = i // (r.span // CHUNK)
+    e, g = spread_heads(), gather_heads()
+    run, dt = r.run[rows, :], r.dtm[rows, :]
+    end = run[CHUNK - 1 : CHUNK]
+    enter = jnp.where(ids == before, jnp.exp(run), 0.0)
+    weight = jnp.where(ids == last, jnp.exp(end - run), 0.0)
+    entx, wx, dtx = mm(enter, e, exact=0), mm(weight, e, exact=0), mm(dt, e, exact=0)
+    bm = r.bc[rows, 0:STATE]
+    dy = r.gg[rows, :]
+    dend = r.y[rows, :] + r.cum[i][0:1] * r.sin[q]
+    xw = x * dtx * wx
+    dxw = fine(bm, dend)
+    inside = r.gx[rows, :]
+    via_w = dxw * xw
+    through = jnp.sum(dend * start, axis=0, keepdims=True) * r.pex[i][0:1]
+    through = jnp.sum(via_w, axis=0, keepdims=True) + through
+    at_end = mm(jnp.broadcast_to(through, (8, XCOLS)), g, exact=0)[0:1]
+    drun = r.drun[rows, :] - mm(r.xdt[rows, :].astype(f32) * inside + via_w, g, exact=0)
+    drun = drun + jnp.where(iota((CHUNK, 128), 0) == CHUNK - 1, at_end, 0.0)
+    triu = (iota((CHUNK, CHUNK), 0) <= iota((CHUNK, CHUNK), 1)).astype(f32)
+    dla = mm(triu, drun, exact=1)
+    dxdt = inside + dxw * wx
+    neg = -jnp.exp(r.hp[1:2])
+    ddt = dla * neg + mm(dxdt * x, g, exact=0)
+    raw = r.dtr[pl.ds(padded, CHUNK), :] + r.hp[0:1]
+    draw = jnp.where(iota((CHUNK, 128), 1) < HL, ddt * jax.nn.sigmoid(raw), 0.0)
+    r.gx[rows, :] = dxdt * dtx + r.hx[0:1] * dy
+    r.gbc[rows, 0:STATE] += fine(xw, dend, ((1,), (1,)))
+    r.gbc[rows, STATE : 2 * STATE] += fine(dy * entx, start, ((1,), (1,)))
+    r.gpc[pl.ds(padded, CHUNK), ACT:CCOLS] = mm(draw, r.chosen[...], ((1,), (1,))).astype(bf16)
+    r.tally[0:1] += jnp.sum(draw, axis=0, keepdims=True)
+    r.tally[1:2] += jnp.sum(dla * (neg * dt), axis=0, keepdims=True)
+
+
+def phase_back_conv(r, q, lt, grad, window, slope):
+    rows = r.span + PAD
+    tile = pl.ds(pl.multiple_of(lt * 128, 128), 128)
+    kern = r.cv[:, tile]
+    ids = r.idc[q * rows + PAD - 8 : (q + 1) * rows, :]
+    gpre = grad * slope
+    sums = []
+    out = jnp.zeros((rows, 128), f32)
+    for k in range(CONVW):
+        first = 8 - MARGIN + k
+        part = gpre
+        if k < MARGIN:
+            part = jnp.where(ids[first : first + r.span] == ids[8:], gpre, 0.0)
+        sums.append(jnp.sum(part * window[first : first + r.span], axis=0, keepdims=True))
+        ahead = PAD - MARGIN + k
+        pieces = [jnp.zeros((ahead, 128), f32), part * kern[k : k + 1]]
+        if rows - ahead - r.span:
+            pieces.append(jnp.zeros((rows - ahead - r.span, 128), f32))
+        out = out + jnp.concatenate(pieces, axis=0)
+    sums.append(jnp.sum(gpre, axis=0, keepdims=True))
+    sums.append(jnp.zeros((3, 128), f32))
+    r.cvgrad[:, tile] += jnp.concatenate(sums, axis=0)
+    r.gpc[q * rows : (q + 1) * rows, tile] = out.astype(bf16)
+
+
+def unit_of(w, rows, aa, bb):
+    return w.at[pl.ds(2 * aa, 2), pl.ds(pl.multiple_of(2 * rows * bb, 16), 2 * rows)]
+
+
+def shard_of(w, rows, aa, cc, bb, ss):
+    return w.at[2 * aa + cc, pl.ds(pl.multiple_of(2 * rows * bb + rows * ss, 16), rows)]
+
+
+def spread(wires, here, size, get, relay=None):
+    a, c, b, s = here
+    n, nx = size["so"], size["dpo"]
+    crossing = []
+
+    def cross(bb, when):
+        slots = {k: wires.slot() for k in range(1, nx)}
+        for k in range(1, nx):
+            wires.start(get(a, bb), get(a, bb), slots[k], (lax.rem(a + k, nx), c, b, s), when)
+        crossing.append((bb, when, slots))
+        if relay is not None:
+            relay(a, bb, when)
+
+    up = {j: wires.slot() for j in range(1, n)}
+    down = {j: wires.slot() for j in range(1, n)}
+    above, below = (a, c, jnp.minimum(b + 1, n - 1), s), (a, c, jnp.maximum(b - 1, 0), s)
+    wires.start(get(a, b), get(a, b), up[1], above, b + 1 < n)
+    wires.start(get(a, b), get(a, b), down[1], below, b > 0)
+    cross(b, None)
+    yield
+    for j in range(1, n):
+        sides = (
+            (up, jnp.maximum(b - j, 0), b - j >= 0, below, above, b + 1 < n),
+            (down, jnp.minimum(b + j, n - 1), b + j < n, above, below, b > 0),
+        )
+        for slots, origin, there, source, target, onward in sides:
+            wires.arrived(get(a, origin), slots[j], source, there)
+            if j + 1 < n:
+                wires.start(get(a, origin), get(a, origin), slots[j + 1], target, there & onward)
+            cross(origin, there)
+        yield
+    for bb, when, slots in crossing:
+        for k in range(1, nx):
+            aa = lax.rem(a + nx - k, nx)
+            wires.arrived(get(aa, bb), slots[k], (aa, c, b, s), when)
+            if relay is not None:
+                relay(aa, bb, when)
+    yield
+
+
+def collect(wires, here, size, get, x, z, close):
+    a, c, b, s = here
+    n, nx = size["so"], size["dpo"]
+    order = [k for k in range(1, n)] + [0]
+    flown, hops = {}, {}
+    for k in order:
+        bb = lax.rem(b + k, n)
+        for h in range(1, nx):
+            flown[k, h] = wires.slot()
+            wires.start(get(lax.rem(a + h, nx), bb), x.at[h - 1, k], flown[k, h], (lax.rem(a + h, nx), c, b, s))
+    yield
+    for k in order:
+        bb = lax.rem(b + k, n)
+        total = get(a, bb)[...].astype(f32)
+        for h in range(1, nx):
+            wires.arrived(x.at[h - 1, k], flown[k, h], (lax.rem(a + nx - h, nx), c, b, s))
+            total = total + x[h - 1, k].astype(f32)
+        x[0, k] = total.astype(bf16)
+        if k > 0:
+            hops[k] = wires.slot()
+            wires.start(x.at[0, k], z.at[k - 1], hops[k], (a, c, bb, s))
+        yield
+    for k in range(1, n):
+        wires.arrived(z.at[k - 1], hops[k], (a, c, lax.rem(b + n - k, n), s))
+    total = x[0, 0].astype(f32)
+    for k in range(1, n):
+        total = total + z[k - 1].astype(f32)
+    close(total)
+    yield
+
+
+def collect_out(wires, here, size, get, x, y, z, out, sends):
+    a, c, b, s = here
+    n, nx = size["so"], size["dpo"]
+    half = y.shape[2]
+    order = [k for k in range(1, n)] + [0]
+    flown, turned, hops = {}, {}, {}
+    part = lambda bb, ss: x.at[0, bb // 2, :, pl.ds(pl.multiple_of(half * ss, 16), half)]
+    for k in order:
+        bb = lax.rem(b + k, n)
+        for h in range(1, nx):
+            flown[k, h] = wires.slot()
+            to = (lax.rem(a + h, nx), c, b, s)
+            sends.append(wires.start(get(lax.rem(a + h, nx), bb), x.at[h - 1, bb // 2], flown[k, h], to, lax.rem(bb, 2) == s))
+    yield
+    for k in order:
+        bb = lax.rem(b + k, n)
+        has = lax.rem(bb, 2) == s
+        for h in range(1, nx):
+            wires.arrived(x.at[h - 1, bb // 2], flown[k, h], (lax.rem(a + nx - h, nx), c, b, s), has)
+
+        @pl.when(has)
+        def _():
+            total = get(a, bb)[...].astype(f32)
+            for h in range(1, nx):
+                total = total + x[h - 1, bb // 2].astype(f32)
+            x[0, bb // 2] = total.astype(bf16)
+
+        turned[k], hops[k] = wires.slot(), wires.slot()
+        wires.start(part(bb, 1 - s), y.at[bb // 2], turned[k], member(here, 1), has)
+        if k > 0:
+            wires.start(part(bb, s), z.at[k - 1], hops[k], (a, c, bb, s), has)
+        yield
+    for k in order:
+        bb = lax.rem(b + k, n)
+        turns = lax.rem(bb, 2) != s
+        wires.arrived(y.at[bb // 2], turned[k], member(here, 1), turns)
+        if k > 0:
+            wires.start(y.at[bb // 2], z.at[k - 1], hops[k], (a, c, bb, s), turns)
+    yield
+    for k in range(1, n):
+        wires.arrived(z.at[k - 1], hops[k], (a, c, lax.rem(b + n - k, n), s))
+
+    def close(own):
+        for h in range(2):
+            total = own[h].astype(f32)
+            for k in range(1, n):
+                total = total + z[k - 1, h].astype(f32)
+            out[:, h * XCOLS : (h + 1) * XCOLS] = total
+
+    pl.when(lax.rem(b, 2) == s)(lambda: close(part(b, s)[...]))
+    pl.when(lax.rem(b, 2) != s)(lambda: close(y[b // 2]))
+    yield
+
+
+def collect_shared(wires, here, size, g, s1, s2, s3, s4, out):
+    a, c, b, s = here
+    n, nx = size["so"], size["dpo"]
+    slots = [wires.slot() for _ in range(2 + nx + n)]
+    wires.start(g.at[pl.ds(2 * (1 - c), 2)], s1, slots[0], member(here, 2))
+    yield
+    wires.arrived(s1, slots[0], member(here, 2))
+    for k in range(2):
+        s1[k] = (s1[k].astype(f32) + g[2 * c + k].astype(f32)).astype(bf16)
+    wires.start(s1.at[1 - s], s2, slots[1], member(here, 1))
+    yield
+    wires.arrived(s2, slots[1], member(here, 1))
+    for k in range(nx):
+        s2[k] = (s2[k].astype(f32) + s1[s, k].astype(f32)).astype(bf16)
+    for h in range(1, nx):
+        to = lax.rem(a + h, nx)
+        wires.start(s2.at[to], s3.at[h - 1], slots[1 + h], (to, c, b, s))
+    yield
+    total = s2[a].astype(f32)
+    for h in range(1, nx):
+        wires.arrived(s3.at[h - 1], slots[1 + h], (lax.rem(a + nx - h, nx), c, b, s))
+        total = total + s3[h - 1].astype(f32)
+    s3[0] = total.astype(bf16)
+    for k in range(1, n):
+        bb = lax.rem(b + k, n)
+        wires.start(s3.at[0, bb], s4.at[k - 1], slots[1 + nx + k], (a, c, bb, s))
+    yield
+    total = s3[0, b].astype(f32)
+    for k in range(1, n):
+        wires.arrived(s4.at[k - 1], slots[1 + nx + k], (a, c, lax.rem(b + n - k, n), s))
+        total = total + s4[k - 1].astype(f32)
+    out[...] = total
+    yield
+
+
+def finish_units(wires, here, rows, z, out):
+    a, c, b, s = here
+    mine = 2 * c + s
+    back = {}
+
+    def close(total):
+        z[0] = total.astype(bf16)
+        out[mine] = z[0, c, pl.ds(pl.multiple_of(rows * s, 16), rows)]
+        for rel in range(1, 4):
+            _, cc, _, ss = member(here, rel)
+            back[rel] = wires.slot()
+            part = z.at[0, cc, pl.ds(pl.multiple_of(rows * ss, 16), rows)]
+            wires.start(part, out.at[mine], back[rel], member(here, rel))
+
+    def wait():
+        for rel in range(1, 4):
+            _, cc, _, ss = member(here, rel)
+            wires.arrived(out.at[2 * cc + ss], back[rel], member(here, rel))
+
+    return close, wait
+
+
+def sum_all(wires, here, size, mine, z, x):
+    a, c, b, s = here
+    n, nx = size["so"], size["dpo"]
+    slots = [wires.slot() for _ in range(n + nx)]
+    z[b] = mine[...]
+    for k in range(1, n):
+        wires.start(mine, z.at[b], slots[k], (a, c, lax.rem(b + k, n), s))
+    yield
+    for k in range(1, n):
+        origin = lax.rem(b + n - k, n)
+        wires.arrived(z.at[origin], slots[k], (a, c, origin, s))
+    total = z[0]
+    for k in range(1, n):
+        total = total + z[k]
+    x[a] = total
+    for h in range(1, nx):
+        wires.start(x.at[a], x.at[a], slots[n + h], (lax.rem(a + h, nx), c, b, s))
+    yield
+    for h in range(1, nx):
+        origin = lax.rem(a + nx - h, nx)
+        wires.arrived(x.at[origin], slots[n + h], (origin, c, b, s))
+    total = x[0]
+    for h in range(1, nx):
+        total = total + x[h]
+    yield total
+
+
+def run_places(size):
+    per = size["so"] // 2
+    width = INNER // (size["dpo"] * 4 * per)
+    return [
+        (2 * cc + ss, (aa * per + bb) * width)
+        for aa in range(size["dpo"]) for cc in range(2) for bb in range(per) for ss in range(2)
+    ], width
+
+
+def class_runs(values, size, m):
+    places, width = run_places(size)
+    return jnp.concatenate([values[:, k * width : (k + 1) * width] for k, (cls, _) in enumerate(places) if cls == m], axis=1)
+
+
+def joined_runs(of_class, size, first, count):
+    places, width = run_places(size)
+    return jnp.concatenate([of_class[m][:, at : at + width] for m, at in places[first // width : (first + count) // width]], axis=1)
+
+
+def device_index(size, here):
+    a, c, b, s = here
+    return (2 * a + c) * (2 * size["so"]) + 2 * b + s
+
+
+def widened(values, rows, columns):
+    if columns > values.shape[1]:
+        values = jnp.concatenate([values, jnp.zeros((values.shape[0], columns - values.shape[1]), f32)], axis=1)
+    if rows > values.shape[0]:
+        values = jnp.concatenate([values, jnp.zeros((rows - values.shape[0], columns), f32)], axis=0)
+    return values
+
+
+def place_smalls(size, here, r):
+    count = size["dpo"] * 4 * size["so"]
+    index = device_index(size, here)
+    depth = r.normed.shape[1]
+    sub = iota((8, 128), 0)
+
+    def placed(tile, total):
+        return pltpu.roll(widened(tile, 8, total), index * (total // count), 1)
+
+    taps = widened(r.conv_w[...].astype(f32), 128, 128).T[0:8]
+    tile = taps + jnp.where(sub == 4, widened(r.conv_b[...].astype(f32), 1, 128), 0.0)
+    conv = placed(tile, XBC)
+    norm = placed(widened(r.norm_in[...].astype(f32), 8, 128), INNER)
+    pre = placed(widened(r.pre_in[...].astype(f32), 8, 128), depth)
+    sub = iota((8, ACT), 0)
+    low = widened(pre[0:1, ACT:], 1, ACT)
+    common = jnp.where(sub == 6, pre[0:1, :ACT], jnp.where(sub == 7, low, 0.0))
+    for m in range(4):
+        own = jnp.concatenate([class_runs(conv[:, :INNER], size, m), conv[:, INNER:]], axis=1)
+        gain = widened(class_runs(norm, size, m)[0:1], 1, ACT)
+        r.cvs[m] = own + jnp.where(sub == 5, gain, common)
+
+
+def final_smalls(size, here, r):
+    count = size["dpo"] * 4 * size["so"]
+    index = device_index(size, here)
+    depth = 2 * XCOLS
+    tiles = [r.os[m] for m in range(4)]
+
+    def taken(values, total):
+        return pltpu.roll(values, total - index * (total // count), 1)[:, 0:128]
+
+    inner = joined_runs([t[:, :XCOLS] for t in tiles], size, 0, INNER)
+    rest = (tiles[0][:, XCOLS:] + tiles[1][:, XCOLS:]) + (tiles[2][:, XCOLS:] + tiles[3][:, XCOLS:])
+    conv = taken(jnp.concatenate([inner, rest], axis=1), XBC)
+    r.smo[0] = conv
+    r.smo[1] = taken(inner, INNER)
+    r.cwo[...] = widened(conv, 128, 128).T[0 : r.cwo.shape[0], 0:CONVW]
+    pre = [jnp.concatenate([t[6:7], t[7:8, : depth - ACT]], axis=1) for t in tiles]
+    r.smo[2] = taken(widened((pre[0] + pre[1]) + (pre[2] + pre[3]), 8, depth), depth)
+    heads = jnp.zeros((8, 128), f32)
+    for m, t in enumerate(tiles):
+        three = jnp.concatenate([t[5:6, XCOLS : XCOLS + 128], t[5:6, XCOLS + 128 :], t[7:8, depth - ACT : depth - ACT + 128]], axis=0)
+        heads = heads + pick_heads(widened(three, 8, 128), class_heads(size, m // 2, m % 2), ((1,), (1,)))
+    r.smo[3] = heads
+
+
+def chain(wires, here, size, r, step):
+    a, c, b, s = here
+    n = size["so"]
+    half = XCOLS // 2
+    to = (a, c, jnp.clip(b + step, 0, n - 1), s)
+    origin = (a, c, jnp.clip(b - step, 0, n - 1), s)
+    place_in = b if step > 0 else n - 1 - b
+    copies = []
+    for m in range(4):
+        slot = wires.slot()
+        copies.append((wires.copy(r.cout.at[m], r.cin.at[m], slot, to), slot))
+        wires.pending.append((copies[m][0], place_in + 1 < n))
+
+    def hop(h):
+        def act():
+            for m in range(4):
+                q, cols = m // 2, slice((m % 2) * half, (m % 2 + 1) * half)
+                if h == 0:
+                    value = r.end[q, :, cols]
+                    r.sin[q, :, cols] = jnp.zeros((STATE, half), f32)
+                else:
+                    wires.arrived(r.cin.at[m], copies[m][1], origin)
+                    value = r.cin[m].astype(f32)
+                    r.sin[q, :, cols] = value
+                    value = r.fac[q, 0:1, cols] * value + r.end[q, :, cols]
+                if h + 1 < n:
+                    r.cout[m] = value.astype(bf16)
+                    copies[m][0].start()
+        pl.when(place_in == h)(act)
+
+    return hop
+
+
+def named(names, refs):
+    return types.SimpleNamespace(**dict(zip(names, refs)))
+
+
+def forward_kernel(size, names, *refs):
+    r = named(names, refs)
+    here = place()
+    a, c, b, s = here
+    n, nx = size["so"], size["dpo"]
+    mine = 2 * c + s
+    own = r.tok.shape[0]
+    r.span = span = 2 * own
+    rows = r.w_in.shape[0]
+    halves = r.wo_in.shape[0]
+    depth = r.toks.shape[1]
+    r.bc = r.act.at[:, XCOLS:ACT]
+    wires = Wires(r.send, r.recv, r.local)
+    follows = (s == 1) & (b + 1 < n)
+    next_group = [(a, cc, jnp.minimum(b + 1, n - 1), ss) for cc in range(2) for ss in range(2)]
+    prior = [(a, cc, jnp.maximum(b - 1, 0), 1) for cc in range(2)]
+    met = greet(here, size, [(next_group, follows), (prior, b > 0)])
+
+    wires.keep(r.w_in, r.wraw)()
+    inner = r.wraw[:, INNER : 2 * INNER].astype(f32)
+    for m in range(4):
+        r.wxs[m] = class_runs(inner, size, m).astype(bf16)
+    shared = widened(r.wraw[:, 2 * INNER :].astype(f32), rows, CCOLS - XCOLS)
+    r.wsr[mine, a, b] = shared.astype(bf16)
+    place_smalls(size, here, r)
+    met()
+
+    first = {}
+
+    def begin(name, src, dst):
+        waits = [wires.keep(src.at[mine], shard_of(dst, rows, a, c, b, s))]
+        for rel in range(1, 4):
+            _, cc, _, ss = member(here, rel)
+            first[name, rel] = wires.slot()
+            wires.start(src.at[2 * cc + ss], shard_of(dst, rows, a, c, b, s), first[name, rel], member(here, rel))
+        return waits[0]
+
+    def began(name, dst, wait):
+        for rel in range(1, 4):
+            _, cc, _, ss = member(here, rel)
+            wires.arrived(shard_of(dst, rows, a, cc, b, ss), first[name, rel], member(here, rel))
+        wait()
+
+    wait_x = begin("x", r.wxs, r.wcx)
+    spread_s = spread(wires, here, size, lambda aa, bb: r.wsr.at[mine, aa, bb])
+    next(spread_s)
+    for rel in range(1, 4):
+        _, cc, _, ss = member(here, rel)
+        first["s", rel] = wires.slot()
+        wires.start(r.cvs.at[2 * cc + ss], r.cvy.at[rel - 1], first["s", rel], member(here, rel))
+    gate = r.wraw[:, 0:INNER].astype(f32)
+    for m in range(4):
+        r.wgs[m] = class_runs(gate, size, m).astype(bf16)
+
+    own_rows = lambda cc, ss: pl.ds(pl.multiple_of(cc * (span + PAD) + PAD + own * ss, 16), own)
+    cot_rows = lambda cc, ss: pl.ds(pl.multiple_of(cc * span + own * ss, 16), own)
+    pairs = {"t": (r.tok, r.toks, own_rows), "k": (r.cot, r.cots, cot_rows)}
+
+    def begin_rows(key):
+        src, dst, at = pairs[key]
+        wait = wires.keep(src, dst.at[at(c, s)])
+        for rel in (1, 2):
+            first[key, rel] = wires.slot()
+            wires.start(src, dst.at[at(c, s)], first[key, rel], member(here, rel))
+        first[key, 3] = wires.slot()
+        return wait
+
+    def pass_rows(key):
+        src, dst, at = pairs[key]
+        wires.arrived(dst.at[at(c, 1 - s)], first[key, 1], member(here, 1))
+        wires.start(dst.at[at(c, 1 - s)], dst.at[at(c, 1 - s)], first[key, 3], member(here, 2))
+
+    def end_rows(key, wait):
+        src, dst, at = pairs[key]
+        for rel, ss in ((2, s), (3, 1 - s)):
+            wires.arrived(dst.at[at(1 - c, ss)], first[key, rel], member(here, 2))
+        wait()
+
+    shares = []
+
+    def share(aa):
+        for rel in range(1, 4):
+            shares.append((aa, rel, wires.slot()))
+            wires.start(r.wsr.at[mine, aa], r.wsr.at[mine, aa], shares[-1][2], member(here, rel))
+
+    began("x", r.wcx, wait_x)
+    spread_x = spread(wires, here, size, lambda aa, bb: unit_of(r.wcx, rows, aa, bb))
+    next(spread_x)
+    wait_t = begin_rows("t")
+    sub = iota((8, 128), 0)
+    places = r.idin[...].astype(f32)
+    tile = jnp.zeros((8, 128), f32)
+    for j in range(own // 128):
+        tile = jnp.where(sub == j, places[:, j * 128 : (j + 1) * 128], tile)
+    r.ids[mine] = tile
+    for rel in range(1, 4):
+        first["i", rel] = wires.slot()
+        wires.start(r.ids.at[mine], r.ids.at[mine], first["i", rel], member(here, rel))
+    halo_rows = lambda cc: pl.ds(pl.multiple_of(cc * (span + PAD), 16), PAD)
+    tail = r.tok.at[own - PAD : own]
+    halo_slots, hid_slots = [wires.slot() for _ in range(4)], [wires.slot() for _ in range(4)]
+    for k, device in enumerate(next_group):
+        wires.start(tail, r.toks.at[halo_rows(c)], halo_slots[k], device, follows, halo_slots[0] + c)
+        wires.start(r.ids.at[mine], r.hid.at[c], hid_slots[k], device, follows, hid_slots[0] + c)
+    wait_g = begin("g", r.wgs, r.wg)
+
+    @pl.when(b == 0)
+    def _():
+        for q in range(2):
+            r.toks[q * (span + PAD) : q * (span + PAD) + PAD, :] = jnp.zeros((PAD, depth), bf16)
+        r.hid[...] = jnp.zeros(r.hid.shape, f32)
+
+    r.chosen[...] = class_heads(size, c, s)
+    raw = jnp.where(sub == 0, widened(r.dtb_in[...], 1, 128), jnp.where(sub == 1, widened(r.alog_in[...], 1, 128), jnp.where(sub == 2, widened(r.skip_in[...], 1, 128), 0.0)))
+    r.hp[...] = pick_heads(raw, r.chosen[...])
+    r.hx[...] = pick_heads(jnp.broadcast_to(r.hp[2:3], (8, 128)), spread_heads())
+
+    for rel in range(1, 4):
+        wires.arrived(r.cvy.at[rel - 1], first["s", rel], member(here, rel))
+    r.cvm[...] = (r.cvs[mine] + r.cvy[0]) + (r.cvy[1] + r.cvy[2])
+    smalls = sum_all(wires, here, size, r.cvm, r.cvz, r.cvx)
+    next(smalls)
+    next(spread_s)
+    next(spread_x)
+    pass_rows("t")
+    next(smalls)
+    next(spread_s)
+    next(spread_x)
+    end_rows("t", wait_t)
+    wait_k = begin_rows("k")
+    for rel in range(1, 4):
+        _, cc, _, ss = member(here, rel)
+        wires.arrived(r.ids.at[2 * cc + ss], first["i", rel], member(here, rel))
+    for sc in range(2):
+        wires.arrived(r.toks.at[halo_rows(sc)], halo_slots[0] + sc, prior[sc], b > 0)
+        wires.arrived(r.hid.at[sc], hid_slots[0] + sc, prior[sc], b > 0)
+    per = own // CHUNK
+    for q in range(2):
+        top = jnp.broadcast_to(r.hid[q, per - 1 : per], (CHUNK, 128)).T[CHUNK - PAD :]
+        r.idc[q * (span + PAD) : q * (span + PAD) + PAD, :] = jnp.where(b > 0, top, -1.0)
+        for ss in range(2):
+            for j in range(per):
+                at = q * (span + PAD) + PAD + ss * own + j * CHUNK
+                r.idc[at : at + CHUNK, :] = jnp.broadcast_to(r.ids[2 * q + ss, j : j + 1], (CHUNK, 128)).T
+    small = next(smalls)
+    r.cv[...] = small
+    r.ng[...] = jnp.broadcast_to(small[5:6, :XCOLS], (8, XCOLS))
+    r.gain1[...] = jnp.broadcast_to(
+        jnp.concatenate([small[6:7], small[7:8, : depth - ACT]], axis=1), (8, depth)
+    )
+    block = (span + PAD) // 3
+    for _ in range(n - 3):
+        next(spread_s)
+    share(a)
+    began("g", r.wg, wait_g)
+    spread_g = spread(wires, here, size, lambda aa, bb: unit_of(r.wg, rows, aa, bb))
+    next(spread_g)
+    loop(6, lambda i: phase_norm(r, i, block))
+    for _ in range(n - 3):
+        next(spread_x)
+    next(spread_s)
+    for h in range(1, nx):
+        share(lax.rem(a + h, nx))
+    next(spread_x)
+    turns = []
+
+    def turn(aa, bb, when):
+        slot = wires.slot()
+        other = lax.rem(bb, 2) != s
+        here_too = lax.rem(bb, 2) == s
+        if when is not None:
+            other, here_too = other & when, here_too & when
+        wires.start(r.wo.at[1, aa, bb // 2, s], r.wo.at[0, aa, bb // 2, s], slot, member(here, 1), other)
+        turns.append((r.wo.at[0, aa, bb // 2, 1 - s], slot, member(here, 1), here_too))
+
+    get_o = lambda aa, bb: r.wo.at[lax.rem(bb + s, 2), aa, bb // 2, s]
+    wires.keep(r.wo_in, get_o(a, b))()
+    spread_o = spread(wires, here, size, get_o, turn)
+    next(spread_o)
+    for aa, rel, slot in shares:
+        _, cc, _, ss = member(here, rel)
+        wires.arrived(r.wsr.at[2 * cc + ss, aa], slot, member(here, rel))
+    for m in range(4):
+        for aa in range(nx):
+            for bb in range(n):
+                at = (2 * bb + m % 2) * rows
+                r.wcs[2 * aa + m // 2, at : at + rows, :] = r.wsr[m, aa, bb]
+    w = r.wcs[:, :, 2 * STATE :]
+    r.dtr[...] = pick_heads(mm(r.normed[...], w.reshape(w.shape[0] * w.shape[1], 128)), r.chosen[...])
+    steps = list(range(1, n))
+    for q in range(2):
+        def columns(ct, q=q):
+            at = pl.multiple_of(ct * 256, 256)
+            phase_in(r, q, r.wcx[:, :, pl.ds(at, 256)], at)
+
+        loop(XCOLS // 256, columns)
+        phase_in(r, q, r.wcs[:, :, 0 : 2 * STATE], XCOLS)
+        if steps:
+            next(spread_g)
+            steps.pop()
+    chunks = 2 * span // CHUNK
+    loop(chunks, lambda i: phase_decay(r, i))
+    phase_states(r)
+    hop = chain(wires, here, size, r, 1)
+    hop(0)
+    while steps:
+        next(spread_g)
+        steps.pop()
+    pass_rows("k")
+    next(spread_o)
+    flushes = [wires.keep(src, dst) for src, dst in ((r.normed, r.normed_o), (r.pc, r.pc_o), (r.sp, r.sp_o), (r.act, r.act_o), (r.xdt, r.xdt_o), (r.wcx, r.wcx_o), (r.wcs, r.wcs_o), (r.dtm, r.dtm_o), (r.run, r.run_o), (r.dtr, r.dtr_o), (r.idc, r.idc_o))]
+
+    def inner_z(q, ct):
+        wide = pl.ds(pl.multiple_of(ct * 256, 256), 256)
+        w = r.wg[:, :, wide]
+        lines = r.normed[q * (span + PAD) + PAD : (q + 1) * (span + PAD), :]
+        r.z[q * span : (q + 1) * span, wide] = mm(lines, w.reshape(w.shape[0] * w.shape[1], 256))
+
+    def fill_a():
+        loop(chunks // 2, lambda i: phase_inside(r, i))
+
+    def fill_b():
+        next(spread_g)
+        for q in range(2):
+            loop(XCOLS // 256, lambda ct, q=q: inner_z(q, ct))
+
+    def fill_c():
+        loop(chunks, lambda i: phase_inside(r, i), chunks // 2)
+
+    fillers = [fill_a, fill_b, fill_c]
+    for h in range(1, n):
+        if fillers:
+            fillers.pop(0)()
+        hop(h)
+        if h < n - 1:
+            next(spread_o)
+    for fill in fillers:
+        fill()
+    end_rows("k", wait_k)
+    flushes += [wires.keep(src, dst) for src, dst in ((r.wg, r.wg_o), (r.z, r.z_o), (r.cots, r.cots_o))]
+    next(spread_o)
+    for landing, slot, device, when in turns:
+        wires.arrived(landing, slot, device, when)
+    flushes.append(wires.keep(r.wo.at[0], r.wo_o))
+    per_x = XCOLS // nx
+
+    def back_product(k):
+        w = r.wo[0, k]
+        r.gg[:, pl.ds(pl.multiple_of(k * per_x, 128), per_x)] = mm(r.cots[...], w.reshape(per_x, depth), ((1,), (1,)))
+
+    loop(nx, back_product)
+    flushes.append(wires.keep(r.gg, r.gg_o))
+    loop(chunks, lambda i: phase_carried(r, i))
+    flushes += [wires.keep(src, dst) for src, dst in ((r.y, r.y_o), (r.st, r.st_o))]
+    wires.finish()
+    for flush in flushes:
+        flush()
+
+
+def backward_kernel(size, names, *refs):
+    r = named(names, refs)
+    here = place()
+    a, c, b, s = here
+    n, nx = size["so"], size["dpo"]
+    mine = 2 * c + s
+    own, depth = r.tok.shape
+    r.span = span = 2 * own
+    rows = r.rest.shape[0]
+    halves = r.oo.shape[0]
+    lines = span + PAD
+    chunks = 2 * span // CHUNK
+    per_dp = r.gg_w.shape[1]
+    half_cols = [slice(k * XCOLS, (k + 1) * XCOLS) for k in range(2)]
+    wires = Wires(r.send, r.recv, r.local)
+    fetched = {}
+    for name in ("y", "z", "gg", "wo", "run", "idc", "normed", "dtm", "dtr", "wg", "wcx", "wcs"):
+        fetched[name] = wires.keep(getattr(r, name + "_i"), getattr(r, name))
+    fetched["bc"] = wires.keep(r.act_i.at[:, XCOLS:ACT], r.bc)
+    fetched["cots"] = wires.keep(r.cots_i, r.cots.at[0 : 2 * span])
+    need = lambda *keys: [fetched.pop(key)() for key in keys]
+    follows = (s == 1) & (b + 1 < n)
+    next_pair = [(a, c, jnp.minimum(b + 1, n - 1), ss) for ss in range(2)]
+    prior = (a, c, jnp.maximum(b - 1, 0), 1)
+    met = greet(here, size, [(next_pair, follows), ([prior], b > 0)])
+    r.gx = r.z
+    r.chosen[...] = class_heads(size, c, s)
+    r.nggrad[...] = jnp.zeros(r.nggrad.shape, f32)
+    r.tally[...] = jnp.zeros(r.tally.shape, f32)
+    r.cvgrad[...] = jnp.zeros(r.cvgrad.shape, f32)
+    for q in range(2):
+        r.gpc[q * lines : q * lines + PAD, :] = jnp.zeros((PAD, CCOLS), bf16)
+
+    need("y", "z", "gg")
+    loop(chunks, lambda i: phase_sums(r, i))
+    met()
+    slots = {}
+    for rel in range(1, 4):
+        slots[rel] = wires.slot()
+        wires.start(r.sums.at[0], r.sums.at[rel], slots[rel], member(here, rel))
+    need("cots", "wo", "bc", "run", "idc")
+    for rel in range(1, 4):
+        wires.arrived(r.sums.at[rel], slots[rel], member(here, rel))
+    loop(chunks, lambda i: phase_gate(r, i))
+
+    def out_grad(k):
+        left = r.gated[:, pl.ds(pl.multiple_of(k * per_dp, 128), per_dp)]
+        for h, cols in enumerate(half_cols):
+            r.go[2 * k + h] = mm(left, r.cots[0 : 2 * span, cols], ((0,), (0,))).astype(bf16)
+
+    loop(nx, out_grad)
+    units_o = 2 * halves
+    get_o = lambda aa, bb: r.go.at[pl.ds(2 * aa, 2), pl.ds(pl.multiple_of((bb // 2) * units_o, 16), units_o)]
+    sends_o = []
+    collect_o = collect_out(wires, here, size, get_o, r.xo, r.yo, r.zo, r.oo, sends_o)
+    next(collect_o)
+
+    x_copy = lambda i, slot: pltpu.make_async_copy(
+        r.act_i.at[pl.ds(pl.multiple_of(i * CHUNK, CHUNK), CHUNK), 0:XCOLS], r.xw.at[slot], r.stream.at[6 + slot]
+    )
+    x_copy(0, 0).start()
+
+    def states_chunk(i):
+        slot = lax.rem(i, 2)
+
+        @pl.when(i + 1 < chunks)
+        def _():
+            x_copy(i + 1, 1 - slot).start()
+
+        x_copy(i, slot).wait()
+        phase_back_states(r, i, r.xw[slot])
+
+    loop(chunks, states_chunk)
+    phase_back_chain(r)
+    hop = chain(wires, here, size, r, -1)
+    hop(0)
+
+    need("normed")
+
+    def gate_grad(k):
+        at = pl.ds(pl.multiple_of(k * per_dp, 128), per_dp)
+        total = jnp.zeros((per_dp, XCOLS), f32)
+        for q in range(2):
+            left = r.normed[q * lines + PAD : (q + 1) * lines, at]
+            total = total + mm(left, r.gpg[q * span : (q + 1) * span, :], ((0,), (0,)))
+        r.gg_w[k] = total.astype(bf16)
+
+    loop(depth // per_dp, gate_grad)
+    close_g, wait_g = finish_units(wires, here, rows, r.zg, r.og)
+    collect_g = collect(wires, here, size, lambda aa, bb: unit_of(r.gg_w, rows, aa, bb), r.xg, r.zg, close_g)
+    next(collect_g)
+
+    def mix(k):
+        tile = pl.ds(pl.multiple_of(k * 256, 256), 256)
+        w = r.wo[:, :, :, :, tile]
+        r.cots[0 : 2 * span, tile] = mm(r.gated[...], w.reshape(XCOLS, 256)).astype(bf16)
+
+    loop(depth // 256, mix)
+    r.xdt = r.gated
+    fetched["xdt"] = wires.keep(r.xdt_i, r.xdt)
+    m_slots = [wires.slot(), wires.slot()]
+    half = lambda cc: pl.ds(pl.multiple_of(cc * span, 16), span)
+    m_sent = wires.start(r.cots.at[half(1 - c)], r.t1.at[0:span], m_slots[0], member(here, 2))
+
+    entries = []
+    need("xdt")
+
+    def fill_a():
+        loop(chunks // 2, lambda i: phase_back_inside(r, i))
+
+    def fill_b():
+        wires.arrived(r.t1.at[0:span], m_slots[0], member(here, 2))
+        at = pl.ds(pl.multiple_of(own * (1 - s), 16), own)
+        r.t1[at, :] = (r.t1[at, :].astype(f32) + r.cots[pl.ds(pl.multiple_of(c * span + own * (1 - s), 16), own), :].astype(f32)).astype(bf16)
+        entries.append(wires.start(r.t1.at[at], r.t2, m_slots[1], member(here, 1)))
+        loop(chunks, lambda i: phase_back_inside(r, i), chunks // 2)
+
+    fillers = [lambda: None, fill_a, fill_b]
+    for h in range(1, n):
+        if fillers:
+            fillers.pop(0)()
+        hop(h)
+    for fill in fillers:
+        fill()
+    for _ in range(n):
+        next(collect_o)
+    need("dtm", "dtr")
+    state_copy = lambda i, slot: pltpu.make_async_copy(r.st_i.at[i], r.stw.at[slot], r.stream.at[4 + slot])
+    state_copy(0, 0).start()
+    x_copy(0, 0).start()
+
+    def close_chunk(i):
+        slot = lax.rem(i, 2)
+
+        @pl.when(i + 1 < chunks)
+        def _():
+            state_copy(i + 1, 1 - slot).start()
+            x_copy(i + 1, 1 - slot).start()
+
+        state_copy(i, slot).wait()
+        x_copy(i, slot).wait()
+        phase_back_close(r, i, r.stw[slot], r.xw[slot])
+
+    quarter = chunks // 4
+    for k in range(4):
+        loop((k + 1) * quarter, close_chunk, k * quarter)
+        if k == 1:
+            next(collect_o)
+        if 0 < k < n - 1:
+            next(collect_g)
+    for k in range(2):
+        fetched["tok", k] = wires.keep(r.tok.at[:, half_cols[k]], r.gated.at[k * own : (k + 1) * own])
+        fetched["cot", k] = wires.keep(r.cot.at[:, half_cols[k]], r.gated.at[(2 + k) * own : (3 + k) * own])
+    wide, narrow = XCOLS // 128, 2 * STATE // 128
+    stream = r.stream
+
+    def tile_place(k):
+        early = k < 2 * wide
+        late = k - 2 * wide
+        return jnp.where(early, k // wide, late // narrow), jnp.where(early, k % wide, wide + late % narrow)
+
+    def tile_copies(k, slot):
+        q, lt = tile_place(k)
+        cols = pl.ds(pl.multiple_of(lt * 128, 128), 128)
+        top = pl.multiple_of(q * lines + PAD - 8, 8)
+        flat = pl.multiple_of(q * span, 16)
+        return (
+            pltpu.make_async_copy(r.pc_i.at[pl.ds(top, span + 8), cols], r.pcw.at[slot], stream.at[2 * slot]),
+            pltpu.make_async_copy(r.sp_i.at[pl.ds(flat, span), cols], r.spw.at[slot], stream.at[2 * slot + 1]),
+        )
+
+    for copy in tile_copies(jnp.int32(0), 0):
+        copy.start()
+
+    def conv_tiles(q, first, count, grads, lead):
+        def conv_tile(k):
+            slot = lax.rem(k, 2)
+
+            @pl.when(k + 1 < 2 * (wide + narrow))
+            def _():
+                for copy in tile_copies(k + 1, 1 - slot):
+                    copy.start()
+
+            for copy in tile_copies(k, slot):
+                copy.wait()
+            lt = k - first
+            grad = grads[q * span : (q + 1) * span, pl.ds(pl.multiple_of(lt * 128, 128), 128)]
+            phase_back_conv(r, q, lt + lead, grad, r.pcw[slot], r.spw[slot])
+
+        loop(first + count, conv_tile, first)
+
+    conv_tiles(0, 0, wide, r.gx, 0)
+    for _ in range(n - 3):
+        next(collect_g)
+    conv_tiles(1, wide, wide, r.gx, 0)
+    for entry in sends_o:
+        wires.sent(entry)
+    r.gcx = r.go
+
+    def in_grad(k):
+        at = pl.ds(pl.multiple_of(k * per_dp, 128), per_dp)
+        r.gcx[k] = mm(r.normed[:, at], r.gpc[:, 0:XCOLS], ((0,), (0,))).astype(bf16)
+
+    def rest_grad(k):
+        at = pl.ds(pl.multiple_of(k * per_dp, 128), per_dp)
+        value = mm(r.normed[:, at], r.gpc[:, XCOLS:CCOLS], ((0,), (0,))).astype(bf16)
+        for bb in range(n):
+            for ss in range(2):
+                first = (2 * bb + ss) * rows
+                r.gs[2 * (k % 2) + ss, k // 2, bb] = value[first : first + rows]
+
+    loop(depth // per_dp, in_grad)
+    close_x, wait_x = finish_units(wires, here, rows, r.zcx, r.ocx)
+    collect_x = collect(wires, here, size, lambda aa, bb: unit_of(r.gcx, rows, aa, bb), r.xcx, r.zcx, close_x)
+    next(collect_x)
+    next(collect_g)
+    conv_tiles(0, 2 * wide, narrow, r.gbc, wide)
+    conv_tiles(1, 2 * wide + narrow, narrow, r.gbc, wide)
+    loop(depth // per_dp, rest_grad)
+    collect_s = collect_shared(wires, here, size, r.gs, r.s1, r.s2, r.s3, r.s4, r.rest)
+    next(collect_s)
+    next(collect_o)
+
+    need(("tok", 0), ("tok", 1), ("cot", 0), ("cot", 1))
+    wires.arrived(r.t2, m_slots[1], member(here, 1))
+    here_rows = pl.ds(pl.multiple_of(c * span + own * s, 16), own)
+    for k, cols in enumerate(half_cols):
+        branch = r.cots[here_rows, cols].astype(f32) + r.t1[pl.ds(pl.multiple_of(own * s, 16), own), cols].astype(f32) + r.t2[:, cols].astype(f32)
+        r.t2[:, cols] = (r.gated[k * own : (k + 1) * own, :].astype(f32) + branch).astype(bf16)
+    wires.keep(r.t2, r.mixed)()
+    wires.sent(m_sent)
+    wires.sent(entries[0])
+    for k, rel in enumerate((2, 1)):
+        pl.semaphore_signal(r.ack.at[k], inc=1, device_id=member(here, rel), device_id_type=MESH)
+
+    need("wg", "wcx", "wcs")
+    next(collect_s)
+
+    def normed_grad(k):
+        cols = pl.ds(pl.multiple_of(k * per_dp, 128), per_dp)
+        for q in range(2):
+            value = mm(r.gpc[q * lines : (q + 1) * lines, 0:XCOLS], r.wcx[k], ((1,), (1,)))
+            value = value + mm(r.gpc[q * lines : (q + 1) * lines, XCOLS:CCOLS], r.wcs[k], ((1,), (1,)))
+            extra = mm(r.gpg[q * span : (q + 1) * span, :], r.wg[k], ((1,), (1,)))
+            value = value + jnp.concatenate([jnp.zeros((PAD, per_dp), f32), extra], axis=0)
+            r.cots[q * lines : (q + 1) * lines, cols] = value.astype(bf16)
+
+    loop(depth // per_dp, normed_grad)
+    next(collect_x)
+    next(collect_s)
+    t_slots = [wires.slot() for _ in range(4)]
+    seq_rows = lambda cc: pl.ds(pl.multiple_of(cc * lines, 16), lines)
+    pl.semaphore_wait(r.ack.at[0], 1)
+    wires.start(r.cots.at[seq_rows(1 - c)], r.t1, t_slots[0], member(here, 2))
+    next(collect_g)
+    wires.arrived(r.t1, t_slots[0], member(here, 2))
+
+    def pair_sum(at, count, cols):
+        ours = r.cots[pl.ds(pl.multiple_of(c * lines + at, 16), count), cols]
+        return ours.astype(f32) + r.t1[pl.ds(pl.multiple_of(at, 16), count), cols].astype(f32)
+
+    tg = r.y
+    other = PAD + own * (1 - s)
+    for k, cols in enumerate(half_cols):
+        tg[k * own : (k + 1) * own, :] = pair_sum(PAD + own * s, own, cols)
+        r.t1[pl.ds(pl.multiple_of(other, 16), own), cols] = pair_sum(other, own, cols).astype(bf16)
+        r.t1[0:PAD, cols] = pair_sum(0, PAD, cols).astype(bf16)
+    pl.semaphore_wait(r.ack.at[1], 1)
+    wires.start(r.t1.at[pl.ds(pl.multiple_of(other, 16), own)], r.t2, t_slots[1], member(here, 1))
+    for ss in range(2):
+        wires.start(r.t1.at[0:PAD], r.th.at[ss], t_slots[2 + ss], prior, (b > 0) & (s == ss))
+    next(collect_x)
+    next(collect_s)
+    wait_g()
+    wires.arrived(r.t2, t_slots[1], member(here, 1))
+    for ss in range(2):
+        wires.arrived(r.th.at[ss], t_slots[2 + ss], next_pair[ss], follows)
+    for k, cols in enumerate(half_cols):
+        tg[k * own : (k + 1) * own, :] += r.t2[:, cols].astype(f32)
+
+        @pl.when(follows)
+        def _():
+            tg[(k + 1) * own - PAD : (k + 1) * own, :] += r.th[0, :, cols].astype(f32) + r.th[1, :, cols].astype(f32)
+
+    next(collect_x)
+    r.pgrad[...] = jnp.zeros(r.pgrad.shape, f32)
+
+    def final(i):
+        at = [pl.ds(pl.multiple_of(k * own + i * 64, 64), 64) for k in range(4)]
+        t = [r.gated[at[k], :].astype(f32) for k in range(2)]
+        g = [tg[at[k], :] for k in range(2)]
+        u = [g[k] * r.gain1[0:1, half_cols[k]] for k in range(2)]
+        row = lambda left, right: jnp.sum(left[0] * right[0] + left[1] * right[1], axis=1, keepdims=True) / depth
+        scale = lax.rsqrt(row(t, t) + EPSILON)
+        tilt = scale * scale * scale * row(u, t)
+        for k in range(2):
+            tg[at[k], :] = r.gated[at[2 + k], :].astype(f32) + scale * u[k] - t[k] * tilt
+            r.pgrad[0:1, half_cols[k]] += jnp.sum(g[k] * t[k] * scale, axis=0, keepdims=True)
+
+    loop(own // 64, final)
+    next(collect_x)
+    next(collect_s)
+    flushes = [wires.keep(tg.at[k * own : (k + 1) * own], r.tgrad.at[:, half_cols[k]]) for k in range(2)]
+    sub = iota((8, ACT), 0)
+    row5 = jnp.concatenate([r.nggrad[0:1], r.tally[0:1], r.tally[1:2]], axis=1)
+    row7 = widened(jnp.concatenate([r.pgrad[0:1, ACT:], r.tally[2:3]], axis=1), 1, ACT)
+    r.cvm[...] = r.cvgrad[...] + jnp.where(sub == 5, row5, 0.0) + jnp.where(sub == 6, r.pgrad[0:1, :ACT], 0.0) + jnp.where(sub == 7, row7, 0.0)
+    smalls = sum_all(wires, here, size, r.cvm, r.cvz, r.cvx)
+    next(smalls)
+    pieces = INNER // XCOLS
+
+    def assemble(classes, first):
+        for p in range(pieces):
+            at = (first + p) * rows
+            joined = joined_runs([classes[m].astype(f32) for m in range(4)], size, p * XCOLS, XCOLS)
+            r.gg[at : at + rows, :] = joined
+            flushes.append(wires.keep(r.gg.at[at : at + rows], r.iw.at[:, (first + p) * XCOLS : (first + p + 1) * XCOLS]))
+
+    assemble(r.og, 0)
+    next(smalls)
+    for _ in range(n - 4):
+        next(collect_x)
+    r.os[mine] = next(smalls)
+    s_slots = {}
+    for rel in range(1, 4):
+        s_slots[rel] = wires.slot()
+        wires.start(r.os.at[mine], r.os.at[mine], s_slots[rel], member(here, rel))
+    next(collect_x)
+    for rel in range(1, 4):
+        _, cc, _, ss = member(here, rel)
+        wires.arrived(r.os.at[2 * cc + ss], s_slots[rel], member(here, rel))
+    final_smalls(size, here, r)
+    wait_x()
+    assemble(r.ocx, pieces)
+    wires.finish()
+    for flush in flushes:
+        flush()
+
+
+def fast_body(size, tokens, segment_ids, pre_gain, in_weight, conv_weight, conv_bias, dt_bias, a_log, skip_gain, norm_gain, out_weight, cotangent):
+    n, nx = size["so"], size["dpo"]
+    tok, cot = tokens[0], cotangent[0]
+    own, depth = tok.shape
+    span = 2 * own
+    rows, halves = in_weight.shape[0], out_weight.shape[0]
+    chunks = 2 * span // CHUNK
+    total, lines = 2 * span, 2 * (span + PAD)
+    dps = 2 * nx
+    per_dp = 2 * n * rows
+    rest = CCOLS - XCOLS
+
+    hbm_state = dict(
+        normed=((lines, depth), bf16), pc=((lines, ACT), f32), sp=((total, ACT), f32), act=((total, ACT), f32),
+        xdt=((total, XCOLS), bf16), wcx=((dps, per_dp, XCOLS), bf16), wcs=((dps, per_dp, rest), bf16), wg=((dps, per_dp, XCOLS), bf16),
+        wo=((nx, n // 2, 2, halves, depth), bf16), cots=((total, depth), bf16), z=((total, XCOLS), f32), gg=((total, XCOLS), f32),
+        y=((total, XCOLS), f32), st=((chunks, STATE, XCOLS), f32), dtm=((total, 128), f32), run=((total, 128), f32),
+        dtr=((lines, 128), f32), idc=((lines, 128), f32),
+    )
+    vmem_state = dict(
+        fac=((2, 8, XCOLS), f32), pex=((chunks, 8, XCOLS), f32), cv=((8, ACT), f32), ng=((8, XCOLS), f32),
+        gain1=((8, depth), f32), hp=((8, 128), f32), hx=((8, XCOLS), f32),
+    )
+    common = dict(
+        cum=((chunks, 8, XCOLS), f32), end=((2, STATE, XCOLS), f32), sin=((2, STATE, XCOLS), f32),
+        cin=((4, STATE, XCOLS // 2), bf16), cout=((4, STATE, XCOLS // 2), bf16),
+        cvm=((8, ACT), f32), cvz=((n, 8, ACT), f32), cvx=((nx, 8, ACT), f32), chosen=((128, 128), bf16),
+    )
+    copies = 100 + 12 * n * nx
+    semaphores = [pltpu.SemaphoreType.DMA((copies,)), pltpu.SemaphoreType.DMA((copies,)), pltpu.SemaphoreType.DMA((40,))]
+    shape = lambda spec: jax.ShapeDtypeStruct(*spec)
+
+    row = lambda v: v[None]
+    inputs = dict(
+        w_in=in_weight, wo_in=out_weight, tok=tok, cot=cot, idin=segment_ids, conv_w=conv_weight, conv_b=row(conv_bias),
+        norm_in=row(norm_gain), pre_in=row(pre_gain), dtb_in=row(dt_bias), alog_in=row(a_log), skip_in=row(skip_gain),
+    )
+    scratch = dict(hbm_state)
+    scratch.update(common)
+    scratch.update(
+        wo=((2, nx, n // 2, 2, halves, depth), bf16), toks=((lines, depth), bf16), ids=((4, 8, 128), f32), hid=((2, 8, 128), f32),
+        cvs=((4, 8, ACT), f32), cvy=((3, 8, ACT), f32), wraw=(in_weight.shape, bf16), wxs=((4, rows, XCOLS), bf16),
+        wgs=((4, rows, XCOLS), bf16), wsr=((4, nx, n, rows, rest), bf16),
+    )
+    names = list(inputs) + [k + "_o" for k in hbm_state] + list(vmem_state) + list(scratch) + ["send", "recv", "local"]
+    outs = pl.pallas_call(
+        functools.partial(forward_kernel, size, names),
+        out_shape=[shape(v) for v in hbm_state.values()] + [shape(v) for v in vmem_state.values()],
+        in_specs=[HBM] * 4 + [VMEM] * 8,
+        out_specs=[HBM] * len(hbm_state) + [VMEM] * len(vmem_state),
+        scratch_shapes=[pltpu.VMEM(*v) for v in scratch.values()] + semaphores,
+        compiler_params=pltpu.CompilerParams(collective_id=1, has_side_effects=True, vmem_limit_bytes=64 * 2**20 - 2**16),
+    )(*inputs.values())
+    held = dict(zip(hbm_state, outs))
+    small = dict(zip(vmem_state, outs[len(hbm_state) :]))
+
+    results = dict(
+        tgrad=((own, depth), f32), mixed=((own, depth), bf16), iw=((rows, 2 * INNER), f32), rest=((rows, rest), f32),
+        oo=((halves, depth), f32), smo=((4, 8, 128), f32), cwo=(conv_weight.shape, f32),
+    )
+    scratch = {k: v for k, v in hbm_state.items() if k not in ("pc", "sp", "cots", "xdt", "st", "act")}
+    scratch.update(common)
+    unit, unit_o = (2, 2 * rows, XCOLS), (2, 2 * halves, XCOLS)
+    scratch.update(
+        cots=((lines, depth), bf16), gbc=((total, 2 * STATE), f32),
+        gated=((total, XCOLS), bf16), gpg=((total, XCOLS), bf16), gpc=((lines, CCOLS), bf16), drun=((total, 128), f32),
+        sums=((4, chunks, 8, 128), f32), nggrad=((8, XCOLS), f32), tally=((8, 128), f32), cvgrad=((8, ACT), f32),
+        pgrad=((8, depth), f32), go=((dps, n * halves, XCOLS), bf16), gg_w=((dps, per_dp, XCOLS), bf16), gs=((4, nx, n, rows, rest), bf16),
+        xcx=((nx - 1, n) + unit, bf16), xg=((nx - 1, n) + unit, bf16), xo=((nx - 1, n // 2) + unit_o, bf16),
+        zcx=((n - 1,) + unit, bf16), zg=((n - 1,) + unit, bf16), zo=((n - 1, 2, halves, XCOLS), bf16), yo=((n // 2, 2, halves, XCOLS), bf16),
+        s1=((2, nx, n, rows, rest), bf16), s2=((nx, n, rows, rest), bf16), s3=((nx - 1, n, rows, rest), bf16), s4=((n - 1, rows, rest), bf16),
+        ocx=((4, rows, XCOLS), bf16), og=((4, rows, XCOLS), bf16), os=((4, 8, ACT), f32),
+        stw=((2, STATE, XCOLS), f32), xw=((2, CHUNK, XCOLS), f32), bc=((total, 2 * STATE), f32), t1=((span + PAD, depth), bf16),
+        t2=((own, depth), bf16), th=((2, PAD, depth), bf16), pcw=((2, span + 8, 128), f32), spw=((2, span, 128), f32),
+    )
+    names = [k + "_i" for k in hbm_state] + ["tok", "cot"] + list(vmem_state) + list(results) + list(scratch)
+    names += ["send", "recv", "local", "stream", "ack"]
+    outs = pl.pallas_call(
+        functools.partial(backward_kernel, size, names),
+        out_shape=[shape(v) for v in results.values()],
+        in_specs=[HBM] * (len(hbm_state) + 2) + [VMEM] * len(vmem_state),
+        out_specs=[HBM] * 3 + [VMEM] * (len(results) - 3),
+        scratch_shapes=[pltpu.VMEM(*v) for v in scratch.values()] + semaphores + [pltpu.SemaphoreType.DMA((8,)), pltpu.SemaphoreType.REGULAR((2,))],
+        compiler_params=pltpu.CompilerParams(collective_id=2, has_side_effects=True, vmem_limit_bytes=64 * 2**20 - 2**16),
+    )(*held.values(), tok, cot, *small.values())
+    out = dict(zip(results, outs))
+    smo = out["smo"]
+    in_weight_grad = jnp.concatenate([out["iw"], out["rest"][:, : in_weight.shape[1] - 2 * INNER]], axis=1)
+    return (
+        out["mixed"][None], out["tgrad"][None], smo[2, 0, : pre_gain.shape[0]], in_weight_grad, out["cwo"], smo[0, 4, : conv_bias.shape[0]],
+        smo[3, 0, :HEADS], smo[3, 1, :HEADS], smo[3, 2, :HEADS], smo[1, 5, : norm_gain.shape[0]], out["oo"],
+    )
+
+
+def specs(dp, seq):
+    both = dp + seq
+    ins = (
+        P(dp, seq, None), P(dp, seq), P(both), P(both, None), P(both, None), P(both),
+        P(), P(), P(), P(both), P(both, None), P(dp, seq, None),
+    )
+    outs = (
+        P(dp, seq, None), P(dp, seq, None), P(both), P(both, None), P(both, None), P(both),
+        P(), P(), P(), P(both), P(both, None),
+    )
+    return ins, outs
+
 
 def solution(mesh):
-    return jax.shard_map(
-        body,
-        mesh=mesh,
-        in_specs=(
-            P("dp", "seq", None),
-            P("dp", "seq"),
-            P(("dp", "seq")),
-            P(("dp", "seq"), None),
-            P(("dp", "seq"), None),
-            P(("dp", "seq")),
-            P(),
-            P(),
-            P(),
-            P(("dp", "seq")),
-            P(("dp", "seq"), None),
-            P("dp", "seq", None),
-        ),
-        out_specs=(
-            P("dp", "seq", None),
-            P("dp", "seq", None),
-            P(("dp", "seq")),
-            P(("dp", "seq"), None),
-            P(("dp", "seq"), None),
-            P(("dp", "seq")),
-            P(),
-            P(),
-            P(),
-            P(("dp", "seq")),
-            P(("dp", "seq"), None),
-        ),
-        check_vma=False,
-    )
+    dp, seq = mesh.shape["dp"], mesh.shape["seq"]
+    fine = Mesh(mesh.devices.reshape(dp // 2, 2, seq // 2, 2), AXES)
+    size = dict(fine.shape)
+
+    def choose(*args):
+        ok = args[0].shape[0] == dp and args[0].shape[1] == seq * GROUP and size["so"] % 2 == 0
+        ok = ok and INNER % (dp * seq * HEADDIM // 2) == 0 and args[3].shape[0] % (dp * seq * 16) == 0 and HEADS % (dp * seq // 2) == 0 and args[3].shape[0] == 2 * XCOLS
+        if ok:
+            ins, outs = specs(AXES[:2], AXES[2:])
+            return jax.shard_map(functools.partial(fast_body, size), mesh=fine, in_specs=ins, out_specs=outs, check_vma=False)(*args)
+        ins, outs = specs(("dp",), ("seq",))
+        return jax.shard_map(whole_body, mesh=mesh, in_specs=ins, out_specs=outs, check_vma=False)(*args)
+
+    return choose

time: 1510 us -> 311 us (0.21)
  waiting for transfers between devices: 931 us -> 0 us
  Pallas kernels: 0 us -> 297 us
  blocking collectives: 185 us -> 0 us
  matrix products: 158 us -> 0 us
  other arithmetic: 99.4 us -> 2.43 us
  starting transfers between devices: 56.4 us -> 0 us
  local copies, waits for them, and re-layouts: 55.2 us -> 9.55 us
  between operations: 21.1 us -> 0.68 us
    ppermute x17 -> x0, waiting for transfers between devices: 438 us -> none  [passed_along(): return lax.ppermute(block, axis, route)]
    reduce_scatter x3 -> x0, waiting for transfers between devices: 300 us -> none  [the longest x1 290 us: body(): lax.psum_scatter(grad_parts[1], 'dp', scatter_dimension=0, tiled=True)]
    pallas_call x0 -> x2, Pallas kernels: none -> 297 us  [the longest x1 163 us: fast_body(): pl.pallas_call(functools.partial(backward_kernel, size, names), out_shape...]
    unnamed x9 -> x0, waiting for transfers between devices: 179 us -> none
    dot_general x20 -> x0, matrix products: 158 us -> none  [the longest x3 53 us: group_math(): inside = jnp.einsum('tsh,shp->thp', mixing, heads_x, precision=HIGHEST)]
    unnamed x3 -> x0, blocking collectives: 83.1 us -> none
    all_gather x1 -> x0, blocking collectives: 61.7 us -> none  [body(): lax.all_gather(shards[2], ('dp', 'seq'), axis=0, tiled=True)]
    ppermute x17 -> x0, starting transfers between devices: 56.1 us -> none  [passed_along(): return lax.ppermute(block, axis, route)]
  transfers between devices with their start and end apart: 24 -> 0, of which waited for: 19 -> 0; matrix products, arithmetic and copies ran while one was open for 20% -> 0% of each run, Pallas kernels for 0% -> 0%
where the time goes in v2:
time: 311 us; the launch traced here: 310 us
  Pallas kernels  297 us (95%)
  local copies, waits for them, and re-layouts  9.55 us (3%)
    pallas_call x1, Pallas kernels, fast_body(): pl.pallas_call(functools.partial(backward_kernel, size, names), out_shape...  163 us
    pallas_call x1, Pallas kernels, fast_body(): pl.pallas_call(functools.partial(forward_kernel, size, names), out_shape=...  134 us

profile of v2, /device:TPU:1, one launch (start us, length us, event | category | flops | bytes accessed | tf_op | source)
XLA Modules:
  0.0 309.7 jit_solution(883336118646807205)
XLA Ops:
  0.6 1.4 copy.23.refs_5_
  2.0 134.5 %shard_map.203 = (bf16[1056,1536]{1,0:T(8,128)(2,1)}, f32[1056,1024]{1,0:T(8,128)}, f32[1024,1024]{1,0:T(8,128)}, f32[1024,1024]{1,0:T(8,128)}, bf16[1024,768]{1...) custom-call(bf16[48,6448]{1,0:T(8,128)(2,1)} %refs_0_.1, ...), custom_call_target="tpu_custom_call" | custom-call | tf_op jit(solution)/shard_map/pallas_call | solution.py:1630
  136.5 162.5 %shard_map.204 = (f32[256,1536]{1,0:T(8,128)}, bf16[256,1536]{1,0:T(8,128)(2,1)}, f32[48,6144]{1,0:T(8,128)}, f32[48,384]{1,0:T(8,128)}, f32[96,1536]{1,0:T(8,12...) custom-call(bf16[1056,1536]{1,0:T(8,128)(2,1)} %get-tuple-element.43.refs_0_, f32[1056,1024]{1,0:T(8,128)} %get-tuple-element.44.refs_1_, ...), custom_call_target="tpu_custom_call" | custom-call | tf_op jit(solution)/shard_map/pallas_call | solution.py:1662
  299.1 0.0 copy-start.1
  299.1 0.0 copy-start
  299.1 1.3 slice_bitcast_fusion.4
  300.4 1.2 slice_bitcast_fusion
  301.6 1.3 slice_bitcast_fusion.1
  302.9 1.5 copy.24
  304.4 2.4 pad_maximum_fusion
  306.8 0.0 copy-done.1
  306.8 0.0 copy-start.2
  306.8 0.9 copy.28
  307.7 0.0 copy-done
  307.7 1.1 copy.29
  308.9 0.0 copy-done.2
  308.9 0.8 copy.30
Async XLA Ops:
  299.1 7.8 %copy-start.1 = (bf16[256,1536]{1,0:T(8,128)(2,1)S(1)}, bf16[256,1536]{1,0:T(8,128)(2,1)}, u32[]{:S(2)}) copy-start(bf16[256,1536]{1,0:T(8,128)(2,1)} %get-tuple-element.68) | copy-start | bytes 2359300
  299.1 8.6 %copy-start = (f32[256,1536]{1,0:T(8,128)S(1)}, f32[256,1536]{1,0:T(8,128)}, u32[]{:S(2)}) copy-start(f32[256,1536]{1,0:T(8,128)} %get-tuple-element.69) | copy-start | bytes 4718596
  306.8 2.0 copy-start.2

commit v3 on v2

--- a/solution.py
+++ b/solution.py
@@ -659,25 +659,39 @@
     return w.at[2 * aa + cc, pl.ds(pl.multiple_of(2 * rows * bb + rows * ss, 16), rows)]
 
 
-def spread(wires, here, size, get, relay=None):
+def spread(wires, here, size, get, turned=None):
     a, c, b, s = here
     n, nx = size["so"], size["dpo"]
-    crossing = []
-
-    def cross(bb, when):
+    crossing, turns = [], []
+    mine = lambda bb: lax.rem(bb, 2) == s
+    both = lambda when, cond: cond if when is None else when & cond
+
+    def cross(where, bb, when):
         slots = {k: wires.slot() for k in range(1, nx)}
         for k in range(1, nx):
-            wires.start(get(a, bb), get(a, bb), slots[k], (lax.rem(a + k, nx), c, b, s), when)
-        crossing.append((bb, when, slots))
-        if relay is not None:
-            relay(a, bb, when)
+            wires.start(where(a, bb), where(a, bb), slots[k], (lax.rem(a + k, nx), c, b, s), when)
+        crossing.append((where, bb, when, slots))
+
+    def pass_on(bb, when):
+        if turned is None:
+            cross(get, bb, when)
+            return
+        slot = wires.slot()
+        wires.start(get(a, bb), turned(a, bb, s), slot, member(here, 1), both(when, jnp.logical_not(mine(bb))))
+        turns.append((bb, both(when, mine(bb)), slot))
+        cross(get, bb, both(when, mine(bb)))
+
+    def turn_back(items):
+        for bb, when, slot in items:
+            wires.arrived(turned(a, bb, 1 - s), slot, member(here, 1), when)
+            cross(lambda aa, other: turned(aa, other, 1 - s), bb, when)
 
     up = {j: wires.slot() for j in range(1, n)}
     down = {j: wires.slot() for j in range(1, n)}
     above, below = (a, c, jnp.minimum(b + 1, n - 1), s), (a, c, jnp.maximum(b - 1, 0), s)
     wires.start(get(a, b), get(a, b), up[1], above, b + 1 < n)
     wires.start(get(a, b), get(a, b), down[1], below, b > 0)
-    cross(b, None)
+    pass_on(b, None)
     yield
     for j in range(1, n):
         sides = (
@@ -688,14 +702,18 @@
             wires.arrived(get(a, origin), slots[j], source, there)
             if j + 1 < n:
                 wires.start(get(a, origin), get(a, origin), slots[j + 1], target, there & onward)
-            cross(origin, there)
+            pass_on(origin, there)
+        early, late = turns[: len(turns) - 2], turns[len(turns) - 2 :]
+        turn_back(early)
+        turns[:] = late
         yield
-    for bb, when, slots in crossing:
+    turn_back(turns)
+    if turned is not None:
+        yield
+    for where, bb, when, slots in crossing:
         for k in range(1, nx):
             aa = lax.rem(a + nx - k, nx)
-            wires.arrived(get(aa, bb), slots[k], (aa, c, b, s), when)
-            if relay is not None:
-                relay(aa, bb, when)
+            wires.arrived(where(aa, bb), slots[k], (aa, c, b, s), when)
     yield
 
 
@@ -1065,14 +1083,20 @@
     shares = []
 
     def share(aa):
-        for rel in range(1, 4):
-            shares.append((aa, rel, wires.slot()))
-            wires.start(r.wsr.at[mine, aa], r.wsr.at[mine, aa], shares[-1][2], member(here, rel))
-
+        slots = {rel: wires.slot() for rel in range(1, 4)}
+        shares.append((aa, slots))
+        for rel in (1, 2):
+            wires.start(r.wsr.at[mine, aa], r.wsr.at[mine, aa], slots[rel], member(here, rel))
+
+    def share_on(aa, slots):
+        theirs = 2 * c + 1 - s
+        wires.arrived(r.wsr.at[theirs, aa], slots[1], member(here, 1))
+        wires.start(r.wsr.at[theirs, aa], r.wsr.at[theirs, aa], slots[3], member(here, 2))
+
+    wait_t = begin_rows("t")
     began("x", r.wcx, wait_x)
     spread_x = spread(wires, here, size, lambda aa, bb: unit_of(r.wcx, rows, aa, bb))
     next(spread_x)
-    wait_t = begin_rows("t")
     sub = iota((8, 128), 0)
     places = r.idin[...].astype(f32)
     tile = jnp.zeros((8, 128), f32)
@@ -1108,12 +1132,17 @@
     next(smalls)
     next(spread_s)
     next(spread_x)
+    next(smalls)
+    for _ in range(n - 2):
+        next(spread_s)
+        next(spread_x)
+    share(a)
+    began("g", r.wg, wait_g)
+    spread_g = spread(wires, here, size, lambda aa, bb: unit_of(r.wg, rows, aa, bb))
+    next(spread_g)
     pass_rows("t")
-    next(smalls)
-    next(spread_s)
-    next(spread_x)
     end_rows("t", wait_t)
-    wait_k = begin_rows("k")
+    share_on(*shares[0])
     for rel in range(1, 4):
         _, cc, _, ss = member(here, rel)
         wires.arrived(r.ids.at[2 * cc + ss], first["i", rel], member(here, rel))
@@ -1135,37 +1164,21 @@
         jnp.concatenate([small[6:7], small[7:8, : depth - ACT]], axis=1), (8, depth)
     )
     block = (span + PAD) // 3
-    for _ in range(n - 3):
-        next(spread_s)
-    share(a)
-    began("g", r.wg, wait_g)
-    spread_g = spread(wires, here, size, lambda aa, bb: unit_of(r.wg, rows, aa, bb))
-    next(spread_g)
     loop(6, lambda i: phase_norm(r, i, block))
-    for _ in range(n - 3):
-        next(spread_x)
     next(spread_s)
     for h in range(1, nx):
         share(lax.rem(a + h, nx))
     next(spread_x)
-    turns = []
-
-    def turn(aa, bb, when):
-        slot = wires.slot()
-        other = lax.rem(bb, 2) != s
-        here_too = lax.rem(bb, 2) == s
-        if when is not None:
-            other, here_too = other & when, here_too & when
-        wires.start(r.wo.at[1, aa, bb // 2, s], r.wo.at[0, aa, bb // 2, s], slot, member(here, 1), other)
-        turns.append((r.wo.at[0, aa, bb // 2, 1 - s], slot, member(here, 1), here_too))
-
     get_o = lambda aa, bb: r.wo.at[lax.rem(bb + s, 2), aa, bb // 2, s]
     wires.keep(r.wo_in, get_o(a, b))()
-    spread_o = spread(wires, here, size, get_o, turn)
+    spread_o = spread(wires, here, size, get_o, lambda aa, bb, ss: r.wo.at[0, aa, bb // 2, ss])
     next(spread_o)
-    for aa, rel, slot in shares:
-        _, cc, _, ss = member(here, rel)
-        wires.arrived(r.wsr.at[2 * cc + ss, aa], slot, member(here, rel))
+    for aa, slots in shares[1:]:
+        share_on(aa, slots)
+    for aa, slots in shares:
+        wires.arrived(r.wsr.at[2 * (1 - c) + s, aa], slots[2], member(here, 2))
+        wires.arrived(r.wsr.at[2 * (1 - c) + 1 - s, aa], slots[3], member(here, 2))
+    wait_k = begin_rows("k")
     for m in range(4):
         for aa in range(nx):
             for bb in range(n):
@@ -1192,7 +1205,6 @@
     while steps:
         next(spread_g)
         steps.pop()
-    pass_rows("k")
     next(spread_o)
     flushes = [wires.keep(src, dst) for src, dst in ((r.normed, r.normed_o), (r.pc, r.pc_o), (r.sp, r.sp_o), (r.act, r.act_o), (r.xdt, r.xdt_o), (r.wcx, r.wcx_o), (r.wcs, r.wcs_o), (r.dtm, r.dtm_o), (r.run, r.run_o), (r.dtr, r.dtr_o), (r.idc, r.idc_o))]
 
@@ -1217,16 +1229,15 @@
     for h in range(1, n):
         if fillers:
             fillers.pop(0)()
+        if h == n - 1:
+            pass_rows("k")
         hop(h)
-        if h < n - 1:
-            next(spread_o)
+        next(spread_o)
     for fill in fillers:
         fill()
     end_rows("k", wait_k)
     flushes += [wires.keep(src, dst) for src, dst in ((r.wg, r.wg_o), (r.z, r.z_o), (r.cots, r.cots_o))]
     next(spread_o)
-    for landing, slot, device, when in turns:
-        wires.arrived(landing, slot, device, when)
     flushes.append(wires.keep(r.wo.at[0], r.wo_o))
     per_x = XCOLS // nx
 
@@ -1320,21 +1331,6 @@
     hop = chain(wires, here, size, r, -1)
     hop(0)
 
-    need("normed")
-
-    def gate_grad(k):
-        at = pl.ds(pl.multiple_of(k * per_dp, 128), per_dp)
-        total = jnp.zeros((per_dp, XCOLS), f32)
-        for q in range(2):
-            left = r.normed[q * lines + PAD : (q + 1) * lines, at]
-            total = total + mm(left, r.gpg[q * span : (q + 1) * span, :], ((0,), (0,)))
-        r.gg_w[k] = total.astype(bf16)
-
-    loop(depth // per_dp, gate_grad)
-    close_g, wait_g = finish_units(wires, here, rows, r.zg, r.og)
-    collect_g = collect(wires, here, size, lambda aa, bb: unit_of(r.gg_w, rows, aa, bb), r.xg, r.zg, close_g)
-    next(collect_g)
-
     def mix(k):
         tile = pl.ds(pl.multiple_of(k * 256, 256), 256)
         w = r.wo[:, :, :, :, tile]
@@ -1369,6 +1365,21 @@
         fill()
     for _ in range(n):
         next(collect_o)
+    need("normed")
+
+    def gate_grad(k):
+        at = pl.ds(pl.multiple_of(k * per_dp, 128), per_dp)
+        total = jnp.zeros((per_dp, XCOLS), f32)
+        for q in range(2):
+            left = r.normed[q * lines + PAD : (q + 1) * lines, at]
+            total = total + mm(left, r.gpg[q * span : (q + 1) * span, :], ((0,), (0,)))
+        r.gg_w[k] = total.astype(bf16)
+
+    loop(depth // per_dp, gate_grad)
+    close_g, wait_g = finish_units(wires, here, rows, r.zg, r.og)
+    collect_g = collect(wires, here, size, lambda aa, bb: unit_of(r.gg_w, rows, aa, bb), r.xg, r.zg, close_g)
+    next(collect_g)
+
     need("dtm", "dtr")
     state_copy = lambda i, slot: pltpu.make_async_copy(r.st_i.at[i], r.stw.at[slot], r.stream.at[4 + slot])
     state_copy(0, 0).start()
@@ -1389,9 +1400,9 @@
     quarter = chunks // 4
     for k in range(4):
         loop((k + 1) * quarter, close_chunk, k * quarter)
-        if k == 1:
+        if k == 2:
             next(collect_o)
-        if 0 < k < n - 1:
+        if k == 3:
             next(collect_g)
     for k in range(2):
         fetched["tok", k] = wires.keep(r.tok.at[:, half_cols[k]], r.gated.at[k * own : (k + 1) * own])
@@ -1435,9 +1446,9 @@
         loop(first + count, conv_tile, first)
 
     conv_tiles(0, 0, wide, r.gx, 0)
+    conv_tiles(1, wide, wide, r.gx, 0)
     for _ in range(n - 3):
         next(collect_g)
-    conv_tiles(1, wide, wide, r.gx, 0)
     for entry in sends_o:
         wires.sent(entry)
     r.gcx = r.go
@@ -1464,6 +1475,7 @@
     loop(depth // per_dp, rest_grad)
     collect_s = collect_shared(wires, here, size, r.gs, r.s1, r.s2, r.s3, r.s4, r.rest)
     next(collect_s)
+    next(collect_g)
     next(collect_o)
 
     need(("tok", 0), ("tok", 1), ("cot", 0), ("cot", 1))

time: 311 us -> 287 us (0.923)
  Pallas kernels: 297 us -> 273 us
    pallas_call x1, Pallas kernels: 134 us -> 111 us  [fast_body(): pl.pallas_call(functools.partial(forward_kernel, size, names), out_shape=...]
where the time goes in v3:
time: 287 us; the launch traced here: 286 us
  Pallas kernels  273 us (95%)
  local copies, waits for them, and re-layouts  9.55 us (3%)
    pallas_call x1, Pallas kernels, fast_body(): pl.pallas_call(functools.partial(backward_kernel, size, names), out_shape...  163 us
    pallas_call x1, Pallas kernels, fast_body(): pl.pallas_call(functools.partial(forward_kernel, size, names), out_shape=...  111 us

profile of v3, /device:TPU:1, one launch (start us, length us, event | category | flops | bytes accessed | tf_op | source)
XLA Modules:
  0.0 286.1 jit_solution(17416443767436514382)
XLA Ops:
  0.6 1.4 copy.23.refs_5_
  2.0 110.6 %shard_map.203 = (bf16[1056,1536]{1,0:T(8,128)(2,1)}, f32[1056,1024]{1,0:T(8,128)}, f32[1024,1024]{1,0:T(8,128)}, f32[1024,1024]{1,0:T(8,128)}, bf16[1024,768]{1...) custom-call(bf16[48,6448]{1,0:T(8,128)(2,1)} %refs_0_.1, ...), custom_call_target="tpu_custom_call" | custom-call | tf_op jit(solution)/shard_map/pallas_call | solution.py:1642
  112.7 162.9 %shard_map.204 = (f32[256,1536]{1,0:T(8,128)}, bf16[256,1536]{1,0:T(8,128)(2,1)}, f32[48,6144]{1,0:T(8,128)}, f32[48,384]{1,0:T(8,128)}, f32[96,1536]{1,0:T(8,12...) custom-call(bf16[1056,1536]{1,0:T(8,128)(2,1)} %get-tuple-element.43.refs_0_, f32[1056,1024]{1,0:T(8,128)} %get-tuple-element.44.refs_1_, ...), custom_call_target="tpu_custom_call" | custom-call | tf_op jit(solution)/shard_map/pallas_call | solution.py:1674
  275.5 0.0 copy-start.1
  275.5 0.0 copy-start
  275.5 1.3 slice_bitcast_fusion.4
  276.9 1.2 slice_bitcast_fusion
  278.1 1.3 slice_bitcast_fusion.1
  279.4 1.5 copy.24
  280.8 2.4 pad_maximum_fusion
  283.3 0.0 copy-done.1
  283.3 0.0 copy-start.2
  283.3 0.9 copy.28
  284.2 0.0 copy-done
  284.2 1.1 copy.29
  285.3 0.0 copy-done.2
  285.3 0.8 copy.30
Async XLA Ops:
  275.5 7.8 %copy-start.1 = (bf16[256,1536]{1,0:T(8,128)(2,1)S(1)}, bf16[256,1536]{1,0:T(8,128)(2,1)}, u32[]{:S(2)}) copy-start(bf16[256,1536]{1,0:T(8,128)(2,1)} %get-tuple-element.68) | copy-start | bytes 2359300
  275.5 8.6 %copy-start = (f32[256,1536]{1,0:T(8,128)S(1)}, f32[256,1536]{1,0:T(8,128)}, u32[]{:S(2)}) copy-start(f32[256,1536]{1,0:T(8,128)} %get-tuple-element.69) | copy-start | bytes 4718596
  283.3 2.0 copy-start.2
